TPU v7x, 128 devices: a whole 4x4x4 slice. The times are simulated.
128 devices in a mesh: mem: 8 (over y_hi, z), space: 16 (over y_lo, x, core).
Axes of the slice: x: 4, y: 4 (y_hi: 2, y_lo: 2; y = y_hi * 2 + y_lo), z: 4, core: 2. Of those that a mesh axis runs over, the one named last changes fastest.
Arguments:
- theta: float32 [256, 64, 64, 128], P('mem', 'space'), may hold values from -1 to 1
- start: float32 [64, 64, 128], P('space'), may hold values from -6 to 6
- sensors: int32 [4096], replicated, may hold values from 0 to 4095
- observed: float32 [4096], P('space'), may hold values from -6 to 6
- noise: float32 [4096, 256], P('space', 'mem'), may hold values from -3 to 3
- variance: float32 [4096], P('space'), may hold values from 0.25 to 4
Outputs:
- updated: float32 [256, 64, 64, 128], P('mem', 'space')
- predicted: float32 [4096, 256], P('space', 'mem')
All inputs are finite; a program needn't handle non-finite values.
Results may differ from a plain program's by a relative error of at most 0.0085.
Values may be sent and summed in bfloat16 or wider, within the bound.
No kernel may reach another device: no remote copies, remote signals or barrier semaphores. Data moves between devices by JAX's collectives and lax.ppermute only.
A program may use at most 192 MiB of HBM per device.

v0:
```python
import math

import jax
import jax.numpy as jnp
from jax import lax
from jax.sharding import PartitionSpec as P

STEPS = 3


step_size = 0.055


def with_halo(block, sides, width):
    for axis, dim in sides:
        count = lax.axis_size(axis)
        forward = [(i, i + 1) for i in range(count - 1)]
        backward = [(target, source) for source, target in forward]
        low = lax.ppermute(
            lax.slice_in_dim(block, block.shape[dim] - width, None, axis=dim), axis, forward
        )
        high = lax.ppermute(lax.slice_in_dim(block, 0, width, axis=dim), axis, backward)
        block = jnp.concatenate([low, block, high], axis=dim)
    return block


def harmonic(left_k, right_k):
    return 2.0 * left_k * right_k / (left_k + right_k)


def face_terms(padded):
    inner_k = padded[:, 1:-1]
    side_pad = jnp.pad(inner_k, ((0, 0), (0, 0), (1, 1), (1, 1)), constant_values=1.0)
    return (
        harmonic(inner_k, padded[:, :-2]),
        harmonic(inner_k, padded[:, 2:]),
        harmonic(inner_k, side_pad[:, :, :-2, 1:-1]),
        harmonic(inner_k, side_pad[:, :, 2:, 1:-1]),
        harmonic(inner_k, side_pad[:, :, 1:-1, :-2]),
        harmonic(inner_k, side_pad[:, :, 1:-1, 2:]),
    )


def advance(padded, face_coef):
    field_now = padded[:, 1:-1]
    side_pad = jnp.pad(field_now, ((0, 0), (0, 0), (1, 1), (1, 1)))
    net_flux = face_coef[0] * (padded[:, :-2] - field_now) + face_coef[1] * (
        padded[:, 2:] - field_now
    )
    net_flux = (
        net_flux
        + face_coef[2] * (side_pad[:, :, :-2, 1:-1] - field_now)
        + face_coef[3] * (side_pad[:, :, 2:, 1:-1] - field_now)
    )
    net_flux = (
        net_flux
        + face_coef[4] * (side_pad[:, :, 1:-1, :-2] - field_now)
        + face_coef[5] * (side_pad[:, :, 1:-1, 2:] - field_now)
    )
    return field_now + step_size * net_flux


def body(theta, start, sensors, observed, noise, variance):
    members, planes, rows_x, rows_y = theta.shape
    log_ext = with_halo(theta, (("space", 1),), 1)
    face_coef = face_terms(jnp.exp(log_ext))
    field_now = jnp.broadcast_to(start[None], theta.shape)
    for step_index in range(STEPS):
        padded = with_halo(field_now, (("space", 1),), 1)
        field_now = advance(padded, face_coef)
    line_sums = jnp.sum(field_now, axis=3).reshape(members, planes * rows_x)
    first_line = lax.axis_index("space") * planes * rows_x
    line_index = first_line + jnp.arange(planes * rows_x, dtype=jnp.int32)
    sensor_table = (sensors[:, None] == line_index[None, :]).astype(jnp.float32)
    partial_value = jnp.dot(sensor_table, line_sums.T, precision=lax.Precision.HIGHEST) / math.sqrt(
        rows_y
    )
    predicted = lax.psum_scatter(partial_value, "space", scatter_dimension=0, tiled=True)
    whole_obs, whole_noise = (
        lax.all_gather(predicted, "mem", axis=1, tiled=True),
        lax.all_gather(noise, "mem", axis=1, tiled=True),
    )
    ensemble = whole_obs.shape[1]
    center = jnp.mean(whole_obs, axis=1, keepdims=True)
    weight = (1.0 / jnp.sqrt(variance))[:, None]
    spread = (whole_obs - center) * weight / math.sqrt(ensemble - 1)
    misfit = (observed[:, None] + whole_noise - whole_obs) * weight
    gram_part = jnp.dot(spread.T, spread, precision=lax.Precision.HIGHEST)
    right_part = jnp.dot(spread.T, misfit, precision=lax.Precision.HIGHEST)
    gram_part, right_part = lax.psum((gram_part, right_part), "space")
    system = gram_part + jnp.eye(ensemble, dtype=jnp.float32)
    factor = jnp.linalg.cholesky(system)
    mixing = jax.scipy.linalg.cho_solve((factor, True), right_part)
    mixing_low = mixing.astype(jnp.bfloat16)
    own_start = lax.axis_index("mem") * members
    fields = theta.astype(jnp.bfloat16).reshape(members, planes * rows_x * rows_y)
    mine_cols = lax.dynamic_slice_in_dim(mixing_low, own_start, members, 1)
    combined = lax.dot_general(
        mine_cols,
        lax.all_gather(fields, "mem", axis=0, tiled=True),
        (((0,), (0,)), ((), ())),
        preferred_element_type=jnp.float32,
    )
    updated = theta + (combined / math.sqrt(ensemble - 1)).reshape(theta.shape)
    return (updated, predicted)


def solution(mesh):
    in_specs = (
        P("mem", "space", None, None),
        P("space", None, None),
        P(),
        P("space"),
        P("space", "mem"),
        P("space"),
    )
    out_specs = (P("mem", "space", None, None), P("space", "mem"))
    return jax.shard_map(body, mesh=mesh, in_specs=in_specs, out_specs=out_specs, check_vma=False)
```

profile of v0, /device:TPU:1, one launch (start us, length us, event | category | flops | bytes accessed | tf_op | source)
XLA Modules:
  0.0 450.7 jit_solution(12113147932084102323)
XLA Ops:
  8.1 1.8 fusion.93
  9.9 4.6 %collective-permute-start = (f32[32,1,64,128]{3,2,1,0:T(8,128)S(1)}, f32[32,1,64,128]{3,2,1,0:T(8,128)S(1)}, u32[]{:S(2)}, u32[]{:S(2)}) collective-permute-start(f32[32,1,64,128]{3,2,1,0:T(8,128)S(1)} %get-tuple-element.26), channel_id=1, source_target_pairs={{0,1},{1,2},{2,3},{3,4},{4,5},{5,6},{6,7},{7,8},{8,9},{9,10},{10,1... | collective-permute-start | bytes 3145736 | tf_op jit(solution)/shard_map/ppermute | solution.py:19
  14.6 1.9 collective-permute-start.1
  16.6 3.6 collective-permute-start.2
  20.4 1.9 collective-permute-start.3
  22.3 4.0 collective-permute-done
  26.3 4.4 collective-permute-done.1
  30.7 1.1 maximum_exponential_fusion
  32.4 5.1 %collective-permute-done.2 = f32[32,1,64,128]{3,2,1,0:T(8,128)S(1)} collective-permute-done((f32[32,1,64,128]{3,2,1,0:T(8,128)S(1)}, f32[32,1,64,128]{3,2,1,0:T(8,128)S(1)}, u32[]{:S(2)}, u32[]{:S(2)}) %collective-permute-start.2) | collective-permute-done | bytes 1048608 | tf_op jit(solution)/shard_map/ppermute | solution.py:19
  37.5 4.4 collective-permute-done.3
  42.4 9.4 %fusion.35 = f32[32,4,64,128]{3,2,1,0:T(8,128)S(1)} fusion(f32[32,4,64,128]{3,2,1,0:T(8,128)S(1)} %broadcast_in_dim.7, f32[32,1,64,128]{3,2,1,0:T(8,128)S(1)} %collective-permute-done.3, f32[32,1,64,128]{3,2,1,0:T(8,128)S(1)} %collective-permute-done.2, f32[32,6,64,128]{3,2,1,0:T(8,128)S(1)} %maximum_exponential_fusion, f32[32,4,64,128]{3,2,1,0:T(8,128)S(1)} %slice.219), kind=kLoop, calls=%fused_computation.56 | loop fusion | flops 42991616 | bytes 27262976 | tf_op jit(solution)/shard_map/add | solution.py:60
  52.1 1.9 collective-permute-start.4
  54.0 2.5 collective-permute-start.5
  56.5 9.2 %collective-permute-done.4 = f32[32,1,64,128]{3,2,1,0:T(8,128)S(1)} collective-permute-done((f32[32,1,64,128]{3,2,1,0:T(8,128)S(1)}, f32[32,1,64,128]{3,2,1,0:T(8,128)S(1)}, u32[]{:S(2)}, u32[]{:S(2)}) %collective-permute-start.4) | collective-permute-done | bytes 1048608 | tf_op jit(solution)/shard_map/ppermute | solution.py:19
  65.7 4.4 collective-permute-done.5
  70.1 9.4 %fusion.7 = f32[32,4,64,128]{3,2,1,0:T(8,128)S(1)} fusion(f32[32,4,64,128]{3,2,1,0:T(8,128)S(1)} %fusion.35, f32[32,1,64,128]{3,2,1,0:T(8,128)S(1)} %collective-permute-done.5, f32[32,1,64,128]{3,2,1,0:T(8,128)S(1)} %collective-permute-done.4, f32[32,6,64,128]{3,2,1,0:T(8,128)S(1)} %maximum_exponential_fusion, f32[32,4,64,128]{3,2,1,0:T(8,128)S(1)} %slice.219), kind=kLoop, calls=%fused_computation.28 | loop fusion | flops 42991616 | bytes 27262976 | tf_op jit(solution)/shard_map/add | solution.py:60
  79.6 2.0 copy-done.4
  81.6 1.1 fusion.91
  82.7 1.9 collective-permute-start.6
  84.6 2.5 collective-permute-start.7
  87.1 9.5 %collective-permute-done.6 = f32[32,1,64,128]{3,2,1,0:T(8,128)S(1)} collective-permute-done((f32[32,1,64,128]{3,2,1,0:T(8,128)}, f32[32,1,64,128]{3,2,1,0:T(8,128)S(1)}, u32[]{:S(2)}, u32[]{:S(2)}) %collective-permute-start.6) | collective-permute-done | bytes 1048608 | tf_op jit(solution)/shard_map/ppermute | solution.py:19
  96.6 4.1 collective-permute-done.7
  100.7 29.6 %fusion.58 = f32[32,4,64]{2,1,0:T(4,128)S(1)} fusion(f32[32,4,64,128]{3,2,1,0:T(8,128)} %copy-done.4, f32[32,1,64,128]{3,2,1,0:T(8,128)S(1)} %collective-permute-done.7, f32[32,1,64,128]{3,2,1,0:T(8,128)S(1)} %collective-permute-done.6, f32[32,6,64,128]{3,2,1,0:T(8,128)} %copy-done, f32[32,4,64,128]{3,2,1,0:T(8,128)} %copy-done.1), kind=kLoop, calls=%fused_computation.91 | loop fusion | flops 44032000 | bytes 23101440 | tf_op jit(solution)/shard_map/reduce_sum | solution.py:71
  130.4 3.0 convolution_multiply_fusion.1
  133.5 29.9 %all_gather.10 = f32[256,256]{0,1:T(8,128)S(1)} all-gather(f32[256,32]{0,1:T(8,128)S(1)} %copy-done.7), channel_id=1, replica_groups=mesh['mem'=8,'space'=16] {'mem'}, dimensions={1}, use_global_device_ids=true | all-gather | bytes 294912 | tf_op jit(solution)/shard_map/all_gather | solution.py:81
  163.4 35.2 %reduce-scatter.2.cloned.1.call-done = f32[256,32]{0,1:T(8,128)} async-done(((f32[4096,32]{0,1:T(8,128)}), f32[256,32]{0,1:T(8,128)}) %reduce-scatter.2.cloned.1.call-update) | async-done | bytes 32784 | tf_op jit(solution)/shard_map/reduce_scatter | solution.py:78
  198.6 28.8 %all_gather.9 = f32[256,256]{0,1:T(8,128)S(1)} all-gather(f32[256,32]{0,1:T(8,128)} %reduce-scatter.2.cloned.1.call-done), channel_id=1, replica_groups=mesh['mem'=8,'space'=16] {'mem'}, dimensions={1}, use_global_device_ids=true | all-gather | bytes 294912 | tf_op jit(solution)/shard_map/all_gather | solution.py:80
  227.5 1.1 fusion.67
  228.6 1.1 fusion.63
  230.0 2.7 convert_element_type.13
  232.7 2.7 copy.14
  235.4 122.0 %all-reduce.8.cloned.1.call-done = (f32[256,256]{1,0:T(8,128)}, f32[256,256]{0,1:T(8,128)}) async-done(((f32[256,256]{1,0:T(8,128)}, f32[256,256]{0,1:T(8,128)}), (f32[256,256]{1,0:T(8,128)}, f32[256,256]{0,1:T(8,128)})) %all-reduce.8.cloned.1.call-update) | async-done | bytes 524304 | tf_op jit(solution)/shard_map/psum | solution.py:90
  357.5 1.0 convert_add_fusion
  358.6 1.0 fusion.62
  359.6 11.7 %cholesky.50 = f32[128,128]{1,0:T(8,128)S(1)} custom-call(f32[128,128]{1,0:T(8,128)S(1)} %cholesky.118), custom_call_target="Cholesky" | custom-call | tf_op jit(solution)/shard_map/jit(cholesky)/cholesky | solution.py:92
  371.4 9.8 %custom-call.18 = f32[1,128,128]{1,2,0:T(8,128)S(1)} custom-call(f32[1,128,128]{2,1,0:T(8,128)S(1)} %get-tuple-element.33), custom_call_target="InvertDiagBlocksLowerTriangular" | custom-call | tf_op jit(solution)/shard_map/jit(cholesky)/cholesky | solution.py:92
  381.7 11.8 %cholesky.105 = f32[128,128]{1,0:T(8,128)S(1)} custom-call(f32[128,128]{1,0:T(8,128)S(1)} %convolution_subtract_fusion.2), custom_call_target="Cholesky" | custom-call | tf_op jit(solution)/shard_map/jit(cholesky)/cholesky | solution.py:92
  393.5 0.7 compare_reduce_fusion
  395.7 4.2 while.1
  395.7 0.7 fusion.105
  396.3 1.4 bitcast_dynamic-update-slice_fusion.2
  398.4 1.4 bitcast_dynamic-update-slice_fusion.2
  399.9 19.7 %custom-call.19 = f32[2,128,128]{1,2,0:T(8,128)S(1)} custom-call(f32[2,128,128]{2,1,0:T(8,128)S(1)} %get-tuple-element.9), custom_call_target="InvertDiagBlocksLowerTriangular" | custom-call | tf_op jit(solution)/shard_map/jit(_cho_solve)/triangular_solve | solution.py:93
  421.3 7.9 %all-gather.2.cloned.1.call-done = bf16[256,32768]{1,0:T(8,128)(2,1)} async-done(((bf16[32,32768]{1,0:T(8,128)(2,1)}), bf16[256,32768]{1,0:T(8,128)(2,1)}) %all-gather.2.cloned.1.call-update) | async-done | bytes 16777232 | tf_op jit(solution)/shard_map/all_gather | solution.py:100
  429.2 8.9 %fusion.59 = f32[4,8,256,128]{3,1,2,0:T(8,128)S(1)} fusion(bf16[256,32768]{1,0:T(8,128)(2,1)} %all-gather.2.cloned.1.call-done, s32[]{:T(128)S(6)} %select_n.8, bf16[128,256]{1,0:T(8,128)(2,1)S(1)} %convolution_convert_fusion, bf16[128,256]{1,0:T(8,128)(2,1)S(1)} %get-tuple-element.36), kind=kOutput, calls=%fused_computation.92 | convolution fusion | flops 537952256 | bytes 21102596 | tf_op jit(solution)/shard_map/dot_general | solution.py:98
  438.1 0.7 copy.12
  438.9 1.4 copy-done.3
  440.3 2.9 add.170
  (57 shorter events, 5.3 us)
Async XLA Ops:
  8.0 8.5 %copy-start.5 = (f32[4,64,128]{2,1,0:T(8,128)S(1)}, f32[4,64,128]{2,1,0:T(8,128)}, u32[]{:S(2)}) copy-start(f32[4,64,128]{2,1,0:T(8,128)} %param.7) | copy-start | bytes 393220
  8.0 190.6 %reduce-scatter.2.cloned.1.call-start = ((), (), s32[]{:S(2)}) async-start(), calls=%async_computation.1 | async-start | bytes 557056 | tf_op jit(solution)/shard_map/reduce_scatter | solution.py:78
  8.1 22.6 %copy-start.2 = (f32[32,4,64,128]{3,2,1,0:T(8,128)S(1)}, f32[32,4,64,128]{3,2,1,0:T(8,128)}, u32[]{:S(2)}) copy-start(f32[32,4,64,128]{3,2,1,0:T(8,128)} %param.6) | copy-start | bytes 12582916
  9.9 16.4 %collective-permute-start = (f32[32,1,64,128]{3,2,1,0:T(8,128)S(1)}, f32[32,1,64,128]{3,2,1,0:T(8,128)S(1)}, u32[]{:S(2)}, u32[]{:S(2)}) collective-permute-start(f32[32,1,64,128]{3,2,1,0:T(8,128)S(1)} %get-tuple-element.26), channel_id=1, source_target_pairs={{0,1},{1,2},{2,3},{3,4},{4,5},{5,6},{6,7},{7,8},{8,9},{9,10},{10,1... | collective-permute-start | bytes 3145736 | tf_op jit(solution)/shard_map/ppermute | solution.py:19
  14.6 16.1 %collective-permute-start.1 = (f32[32,1,64,128]{3,2,1,0:T(8,128)S(1)}, f32[32,1,64,128]{3,2,1,0:T(8,128)S(1)}, u32[]{:S(2)}, u32[]{:S(2)}) collective-permute-start(f32[32,1,64,128]{3,2,1,0:T(8,128)S(1)} %get-tuple-element.27), channel_id=1, source_target_pairs={{1,0},{2,1},{3,2},{4,3},{5,4},{6,5},{7,6},{8,7},{9,8},{10,9},{11,1... | collective-permute-start | bytes 3145736 | tf_op jit(solution)/shard_map/ppermute | solution.py:22
  16.6 20.9 %collective-permute-start.2 = (f32[32,1,64,128]{3,2,1,0:T(8,128)S(1)}, f32[32,1,64,128]{3,2,1,0:T(8,128)S(1)}, u32[]{:S(2)}, u32[]{:S(2)}) collective-permute-start(f32[32,1,64,128]{3,2,1,0:T(8,128)S(1)} %broadcast_in_dim.8), channel_id=1, source_target_pairs={{0,1},{1,2},{2,3},{3,4},{4,5},{5,6},{6,7},{7,8},{8,9},{9,10},{10,1... | collective-permute-start | bytes 3145736 | tf_op jit(solution)/shard_map/ppermute | solution.py:19
  20.4 21.5 %collective-permute-start.3 = (f32[32,1,64,128]{3,2,1,0:T(8,128)S(1)}, f32[32,1,64,128]{3,2,1,0:T(8,128)S(1)}, u32[]{:S(2)}, u32[]{:S(2)}) collective-permute-start(f32[32,1,64,128]{3,2,1,0:T(8,128)S(1)} %broadcast_in_dim.9), channel_id=1, source_target_pairs={{1,0},{2,1},{3,2},{4,3},{5,4},{6,5},{7,6},{8,7},{9,8},{10,9},{11,1... | collective-permute-start | bytes 3145736 | tf_op jit(solution)/shard_map/ppermute | solution.py:22
  31.8 38.4 %copy-start = (f32[32,6,64,128]{3,2,1,0:T(8,128)}, f32[32,6,64,128]{3,2,1,0:T(8,128)S(1)}, u32[]{:S(2)}) copy-start(f32[32,6,64,128]{3,2,1,0:T(8,128)S(1)} %maximum_exponential_fusion) | copy-start | bytes 18874372
  32.4 37.8 %copy-start.1 = (f32[32,4,64,128]{3,2,1,0:T(8,128)}, f32[32,4,64,128]{3,2,1,0:T(8,128)S(1)}, u32[]{:S(2)}) copy-start(f32[32,4,64,128]{3,2,1,0:T(8,128)S(1)} %slice.219) | copy-start | bytes 12582916
  52.1 13.7 %collective-permute-start.4 = (f32[32,1,64,128]{3,2,1,0:T(8,128)S(1)}, f32[32,1,64,128]{3,2,1,0:T(8,128)S(1)}, u32[]{:S(2)}, u32[]{:S(2)}) collective-permute-start(f32[32,1,64,128]{3,2,1,0:T(8,128)S(1)} %get-tuple-element.24), channel_id=1, source_target_pairs={{0,1},{1,2},{2,3},{3,4},{4,5},{5,6},{6,7},{7,8},{8,9},{9,10},{10,1... | collective-permute-start | bytes 3145736 | tf_op jit(solution)/shard_map/ppermute | solution.py:19
  54.0 16.1 %collective-permute-start.5 = (f32[32,1,64,128]{3,2,1,0:T(8,128)S(1)}, f32[32,1,64,128]{3,2,1,0:T(8,128)S(1)}, u32[]{:S(2)}, u32[]{:S(2)}) collective-permute-start(f32[32,1,64,128]{3,2,1,0:T(8,128)S(1)} %get-tuple-element.25), channel_id=1, source_target_pairs={{1,0},{2,1},{3,2},{4,3},{5,4},{6,5},{7,6},{8,7},{9,8},{10,9},{11,1... | collective-permute-start | bytes 3145736 | tf_op jit(solution)/shard_map/ppermute | solution.py:22
  79.5 2.0 copy-start.4
  82.7 14.0 %collective-permute-start.6 = (f32[32,1,64,128]{3,2,1,0:T(8,128)}, f32[32,1,64,128]{3,2,1,0:T(8,128)S(1)}, u32[]{:S(2)}, u32[]{:S(2)}) collective-permute-start(f32[32,1,64,128]{3,2,1,0:T(8,128)} %get-tuple-element.22), channel_id=1, source_target_pairs={{0,1},{1,2},{2,3},{3,4},{4,5},{5,6},{6,7},{7,8},{8,9},{9,10},{10,1... | collective-permute-start | bytes 3145736 | tf_op jit(solution)/shard_map/ppermute | solution.py:19
  84.6 16.1 %collective-permute-start.7 = (f32[32,1,64,128]{3,2,1,0:T(8,128)S(1)}, f32[32,1,64,128]{3,2,1,0:T(8,128)S(1)}, u32[]{:S(2)}, u32[]{:S(2)}) collective-permute-start(f32[32,1,64,128]{3,2,1,0:T(8,128)S(1)} %get-tuple-element.23), channel_id=1, source_target_pairs={{1,0},{2,1},{3,2},{4,3},{5,4},{6,5},{7,6},{8,7},{9,8},{10,9},{11,1... | collective-permute-start | bytes 3145736 | tf_op jit(solution)/shard_map/ppermute | solution.py:22
  87.1 43.3 %copy-start.10 = (s32[4096]{0:T(1024)S(1)}, s32[4096]{0:T(1024)}, u32[]{:S(2)}) copy-start(s32[4096]{0:T(1024)} %param.8) | copy-start | bytes 49156
  87.1 46.3 %copy-start.8 = (f32[256]{0:T(256)S(1)}, f32[256]{0:T(256)}, u32[]{:S(2)}) copy-start(f32[256]{0:T(256)} %param.11) | copy-start | bytes 3076
  87.1 46.3 %copy-start.7 = (f32[256,32]{0,1:T(8,128)S(1)}, f32[256,32]{0,1:T(8,128)}, u32[]{:S(2)}) copy-start(f32[256,32]{0,1:T(8,128)} %param.10) | copy-start | bytes 98308
  87.1 141.5 %copy-start.9 = (f32[256]{0:T(256)S(1)}, f32[256]{0:T(256)}, u32[]{:S(2)}) copy-start(f32[256]{0:T(256)} %param.9) | copy-start | bytes 3076
  133.4 224.1 %all-reduce.8.cloned.1.call-start = ((), (), s32[]{:S(2)}) async-start(), calls=%async_computation.3 | async-start | bytes 1048576 | tf_op jit(solution)/shard_map/psum | solution.py:90
  229.8 199.4 %all-gather.2.cloned.1.call-start = ((), (), s32[]{:S(2)}) async-start(), calls=%async_computation.2 | async-start | bytes 18874368 | tf_op jit(solution)/shard_map/all_gather | solution.py:100
  357.5 62.1 %copy-start.6 = (f32[256,256]{1,0:T(8,128)S(1)}, f32[256,256]{1,0:T(8,128)}, u32[]{:S(2)}) copy-start(f32[256,256]{1,0:T(8,128)} %get-tuple-element.18) | copy-start | bytes 786436
  438.1 2.2 copy-start.3
Sparse Core Ops, SparseCore 0:
  133.5 65.0 reduce-scatter.1
  229.9 127.5 all-reduce.7
Sparse Core Ops, SparseCore 1:
  235.5 193.7 all-gather.1
where the time goes:
time: 451 us
  waiting for transfers between devices  210 us (47%)
  other arithmetic  111 us (25%)
  blocking collectives  58.7 us (13%)
  starting transfers between devices  21.2 us (5%)
  between operations  17.3 us (4%)
  matrix products  16.3 us (4%)
  local copies, waits for them, and re-layouts  15.9 us (4%)
    psum x1, waiting for transfers between devices, body(): gram_part, right_part = lax.psum((gram_part, right_part), 'space')  122 us
    reduce_scatter x1, waiting for transfers between devices, body(): lax.psum_scatter(partial_value, 'space', scatter_dimension=0, tiled=True)  35.2 us
    another operation x6, other arithmetic, body(): factor = jnp.linalg.cholesky(system)  34.1 us
    all_gather x1, blocking collectives, body(): lax.all_gather(noise, 'mem', axis=1, tiled=True)  29.9 us
    reduce_sum x1, other arithmetic, body(): line_sums = jnp.sum(field_now, axis=3).reshape(members, planes * rows_x)  29.6 us
    all_gather x1, blocking collectives, body(): lax.all_gather(predicted, 'mem', axis=1, tiled=True)  28.8 us
    ppermute x4, waiting for transfers between devices, with_halo(): lax.ppermute(lax.slice_in_dim(block, block.shape[dim] - width, None, axis...  27.8 us
    another operation x3, other arithmetic, body(): mixing = jax.scipy.linalg.cho_solve((factor, True), right_part)  19.7 us
  transfers between devices with their start and end apart: 11, of which 11 were waited for; matrix products, arithmetic and copies ran while one was open for 15% of the time, Pallas kernels for 0%

commit v1 on v0

v1 whole, which is shorter than its diff:
```python
import functools
import math

import jax
import jax.numpy as jnp
from jax import lax
from jax.experimental import pallas as pl
from jax.experimental.pallas import tpu as pltpu
from jax.sharding import PartitionSpec as P

STEPS = 3
STEP_SIZE = 0.055
OUTSIDE = 1.0 / (2.0 * STEP_SIZE)
HIGH = lax.Precision.HIGHEST
NT = (((1,), (1,)), ((), ()))
MIB = 1 << 20


def inverse(x):
    guess = pl.reciprocal(x, approx=True)
    return guess * (2.0 - x * guess)


def diffuse_kernel(edge_ref, theta_ref, low_ref, high_ref, start_ref, out_ref, cx, cy, cz, keep, u1, u2, u3):
    members, planes, rows, lanes = theta_ref.shape
    width = low_ref.shape[1]
    total = planes + 2 * width
    row_at = lax.broadcasted_iota(jnp.int32, (rows, lanes), 0)
    lane_at = lax.broadcasted_iota(jnp.int32, (rows, lanes), 1)
    last_row, last_lane = row_at == rows - 1, lane_at == lanes - 1
    sides = (
        (row_at == 0).astype(jnp.float32)
        + last_row.astype(jnp.float32)
        + (lane_at == 0).astype(jnp.float32)
        + last_lane.astype(jnp.float32)
    )
    low_edge, high_edge = edge_ref[0], edge_ref[1]

    def up(v, axis):
        return pltpu.roll(v, v.shape[axis] - 1, axis)

    def down(v, axis):
        return pltpu.roll(v, 1, axis)

    @pl.loop(0, members)
    def _(m):
        def resistance(p):
            if p < width:
                t = low_ref[m, p].astype(jnp.float32)
            elif p < width + planes:
                t = theta_ref[m, p - width]
            else:
                t = high_ref[m, p - width - planes].astype(jnp.float32)
            return jnp.exp(math.log(OUTSIDE) - t)

        fields = [start_ref, u1, u2, u3]
        flux_z = [None] * STEPS

        def advance(step, p):
            source = fields[step]
            u = source[p]
            if flux_z[step] is None:
                flux_z[step] = cz[p - 1] * (u - source[p - 1])
            fx = cx[p] * (up(u, 0) - u)
            fy = cy[p] * (up(u, 1) - u)
            fz = cz[p] * (source[p + 1] - u)
            new = keep[p] * u + ((fx - down(fx, 0)) + (fy - down(fy, 1)) + (fz - flux_z[step]))
            flux_z[step] = fz
            if p < width:
                new = new * low_edge
            elif p >= width + planes:
                new = new * high_edge
            if step == STEPS - 1:
                u3[p - width] = new
            else:
                fields[step + 1][p] = new

        before = None
        for p in range(total):
            r = resistance(p)
            if before is not None:
                cz[p - 1] = inverse(before + r)
            before = r
            if 1 <= p < total - 1:
                cx[p] = jnp.where(last_row, 0.0, inverse(r + up(r, 0)))
                cy[p] = jnp.where(last_lane, 0.0, inverse(r + up(r, 1)))
                keep[p] = 1.0 - sides * inverse(r + OUTSIDE)
            for step in range(STEPS):
                q = p - 1 - step
                if step + 1 <= q < total - 1 - step:
                    advance(step, q)
        ones = jnp.ones((8, lanes), jnp.float32)
        sums = lax.dot_general(
            ones, u3[...].reshape(planes * rows, lanes), NT, precision=HIGH, preferred_element_type=jnp.float32
        )
        out_ref[pl.ds(m, 1), :] = sums[0:1]


def diffuse(theta, low, high, start_ext, edges):
    members, planes, rows, lanes = theta.shape
    width = low.shape[1]
    total = planes + 2 * width
    some = 8
    shape = (total, rows, lanes)
    return pl.pallas_call(
        diffuse_kernel,
        grid=(members // some,),
        in_specs=[
            pl.BlockSpec(memory_space=pltpu.SMEM),
            pl.BlockSpec((some, planes, rows, lanes), lambda i: (i, 0, 0, 0)),
            pl.BlockSpec((some, width, rows, lanes), lambda i: (i, 0, 0, 0)),
            pl.BlockSpec((some, width, rows, lanes), lambda i: (i, 0, 0, 0)),
            pl.BlockSpec(shape, lambda i: (0, 0, 0)),
        ],
        out_specs=pl.BlockSpec((some, planes * rows), lambda i: (i, 0)),
        out_shape=jax.ShapeDtypeStruct((members, planes * rows), jnp.float32),
        scratch_shapes=[pltpu.VMEM(shape, jnp.float32)] * 6 + [pltpu.VMEM((planes, rows, lanes), jnp.float32)],
        compiler_params=pltpu.CompilerParams(vmem_limit_bytes=24 * MIB),
        cost_estimate=pl.CostEstimate(flops=300 * theta.size, bytes_accessed=8 * theta.size, transcendentals=12 * theta.size),
        name="diffuse",
    )(edges, theta, low, high, start_ext)


def gram_kernel(scale, lines_ref, own_ref, data_ref, out_ref):
    everyone, count = lines_ref.shape
    members = own_ref.shape[0]
    value = lines_ref[...] * scale
    dev = value - jnp.mean(value, axis=0, keepdims=True)
    weight = data_ref[members : members + 1, :]
    left = jnp.concatenate(
        [
            dev * (weight * (1.0 / (everyone - 1))),
            (data_ref[0:members, :] - weight * (own_ref[...] * scale)) * (1.0 / math.sqrt(everyone - 1)),
        ],
        axis=0,
    )
    both = lax.dot_general(left, dev, NT, precision=HIGH, preferred_element_type=jnp.float32)
    chunks, depth, _ = out_ref.shape
    a, b = everyone // chunks, members // chunks
    pad = jnp.zeros((depth - a - b, everyone), jnp.float32)
    for c in range(chunks):
        out_ref[c, 0:a] = both[a * c : a * (c + 1)]
        out_ref[c, a : a + b] = both[everyone + b * c : everyone + b * (c + 1)]
        out_ref[c, a + b :] = pad


def invert_block(block):
    size = block.shape[0]
    lane_at = lax.broadcasted_iota(jnp.int32, (1, size), 1)
    row_at = lax.broadcasted_iota(jnp.int32, (8, 1), 0)
    groups = [block[8 * g : 8 * g + 8] for g in range(size // 8)]
    for k in range(size):
        g, s = divmod(k, 8)
        here = lane_at == k
        pivot_row = groups[g][s : s + 1]
        d = 1.0 / pivot_row[:, k : k + 1]
        row = jnp.where(here, d, pivot_row * d)
        new = []
        for i, rows in enumerate(groups):
            col = rows[:, k : k + 1]
            next_rows = jnp.where(here, 0.0, rows) - col * row
            if i == g:
                next_rows = jnp.where(row_at == s, row, next_rows)
            new.append(next_rows)
        groups = new
    return jnp.concatenate(groups, axis=0)


def solve_kernel(parts_ref, target_ref, out_ref, work, inv):
    chunks, depth, size = parts_ref.shape
    a = size // chunks
    b = depth_rows = out_ref.shape[0] // chunks
    half = size // 2
    rhs = []
    for c in range(chunks):
        work[a * c : a * (c + 1)] = parts_ref[c, 0:a]
        rhs.append(parts_ref[c, a : a + b])
    rhs = jnp.concatenate(rhs, axis=0)
    eye = (
        lax.broadcasted_iota(jnp.int32, (half, half), 0) == lax.broadcasted_iota(jnp.int32, (half, half), 1)
    ).astype(jnp.float32)
    work[0:half, 0:half] += eye
    work[half:, half:] += eye
    dot = functools.partial(jnp.dot, precision=HIGH, preferred_element_type=jnp.float32)

    @pl.loop(0, 2)
    def _(i):
        at = pl.ds(pl.multiple_of(i * half, half), half)

        @pl.when(i == 1)
        def _():
            cross = dot(work[half:, 0:half], inv[0])
            work[half:, half:] = work[half:, half:] - dot(cross, work[0:half, half:])

        inv[i] = invert_block(work[at, at])

    cross = dot(work[half:, 0:half], inv[0])
    first = dot(rhs[:, 0:half], inv[0])
    second = dot(rhs[:, half:] - dot(first, work[0:half, half:]), inv[1])
    first = first - dot(second, cross)
    mixing = jnp.concatenate([first, second], axis=1).astype(jnp.bfloat16)
    order = (lax.broadcasted_iota(jnp.int32, (size, size), 0) == target_ref[...]).astype(jnp.float32).astype(jnp.bfloat16)
    out_ref[...] = jnp.dot(mixing, order, preferred_element_type=jnp.float32).astype(jnp.bfloat16)


def combine_kernel(scale, mix_ref, theta_ref, *refs):
    blocks, out_ref = refs[:-1], refs[-1]
    everyone = jnp.concatenate([ref[...] for ref in blocks], axis=0)
    result = jnp.dot(mix_ref[...], everyone, preferred_element_type=jnp.float32) * scale
    members, rows, lanes = theta_ref.shape
    for r in range(rows):
        out_ref[:, r, :] = theta_ref[:, r, :] + result[:, r * lanes : (r + 1) * lanes]


def combine(mix, theta, blocks):
    members, planes, rows, lanes = theta.shape
    flat = theta.reshape(members, planes * rows, lanes)
    everyone = sum(block.shape[0] for block in blocks)
    some = 16
    out = pl.pallas_call(
        functools.partial(combine_kernel, 1.0 / math.sqrt(everyone - 1)),
        grid=(planes * rows // some,),
        in_specs=[
            pl.BlockSpec(mix.shape, lambda i: (0, 0)),
            pl.BlockSpec((members, some, lanes), lambda i: (0, i, 0)),
        ]
        + [pl.BlockSpec((block.shape[0], some * lanes), lambda i: (0, i)) for block in blocks],
        out_specs=pl.BlockSpec((members, some, lanes), lambda i: (0, i, 0)),
        out_shape=jax.ShapeDtypeStruct(flat.shape, jnp.float32),
        compiler_params=pltpu.CompilerParams(vmem_limit_bytes=24 * MIB),
        cost_estimate=pl.CostEstimate(flops=2 * everyone * theta.size, bytes_accessed=24 * theta.size // 1, transcendentals=0),
        name="combine",
    )(mix, flat, *blocks)
    return out.reshape(theta.shape)


def spread_out(block, axis):
    count = lax.axis_size(axis)
    return lax.all_to_all(jnp.broadcast_to(block[None], (count,) + block.shape), axis, 0, 0)


def body(theta, start, sensors, observed, noise, variance):
    members, planes, rows, lanes = theta.shape
    spaces, mems = lax.axis_size("space"), lax.axis_size("mem")
    lines_here = planes * rows
    mine, me = lax.axis_index("space"), lax.axis_index("mem")
    width = STEPS
    low_theta = theta.astype(jnp.bfloat16)
    forward = [(i, i + 1) for i in range(spaces - 1)]
    backward = [(i + 1, i) for i in range(spaces - 1)]
    theta_low = lax.ppermute(low_theta[:, planes - width :], "space", forward)
    theta_high = lax.ppermute(low_theta[:, :width], "space", backward)
    start_low = lax.ppermute(start[planes - width :], "space", forward)
    start_high = lax.ppermute(start[:width], "space", backward)
    start_ext = jnp.concatenate([start_low, start, start_high], axis=0)
    edges = jnp.stack([mine > 0, mine < spaces - 1]).astype(jnp.float32)

    ring = mems // 2
    along = lambda k: [(i, (i // ring) * ring + (i + k) % ring) for i in range(mems)]
    across = [(i, (i + ring) % mems) for i in range(mems)]
    own = low_theta.reshape(members, lines_here * lanes)
    z_low = lax.ppermute(own, "mem", along(1))
    z_high = lax.ppermute(own, "mem", along(ring - 1))
    theta_low, theta_high, start_ext, own_y = lax.optimization_barrier((theta_low, theta_high, start_ext, own))
    y_own = lax.ppermute(own_y, "mem", across)

    line_at = jnp.arange(spaces * lines_here, dtype=jnp.int32)
    rows_here = observed.shape[0]
    sensors_here = lax.dynamic_slice_in_dim(sensors, mine * rows_here, rows_here, 0)
    pick = (sensors_here[:, None] == line_at[None, :]).astype(jnp.float32)
    inv_var = 1.0 / variance
    data = jnp.concatenate([(observed[None, :] + noise.T) * inv_var[None, :], inv_var[None, :]], axis=0)
    data = jnp.pad(data, ((0, 7), (0, 0)))
    by_line = jnp.dot(data, pick, precision=HIGH).reshape(members + 8, spaces, lines_here).transpose(1, 0, 2)
    by_line = jnp.sum(lax.all_to_all(by_line, "space", 0, 0), axis=0)

    lines = diffuse(theta, theta_low, theta_high, start_ext, edges)
    everyone = members * mems
    lines_all = spread_out(lines, "mem").reshape(everyone, lines_here)
    scale = 1.0 / math.sqrt(lanes)
    depth = 24
    partial_sums = pl.pallas_call(
        functools.partial(gram_kernel, scale),
        out_shape=jax.ShapeDtypeStruct((spaces, depth, everyone), jnp.float32),
        compiler_params=pltpu.CompilerParams(vmem_limit_bytes=16 * MIB),
        name="gram",
    )(lines_all, lines, by_line)
    sums = jnp.sum(lax.all_to_all(partial_sums, "space", 0, 0), axis=0)
    whole = spread_out(sums, "space")

    half = members // 2
    z_low, z_high, _ = lax.optimization_barrier((z_low, z_high, lines))
    far_a = lax.ppermute(z_low[:half], "mem", along(1))
    far_b = lax.ppermute(z_high[half:], "mem", along(ring - 1))
    y_low = lax.ppermute(y_own, "mem", along(1))
    y_high = lax.ppermute(y_own, "mem", along(ring - 1))
    y_far_a = lax.ppermute(far_a, "mem", across)
    y_far_b = lax.ppermute(far_b, "mem", across)

    lines_slabs = spread_out(lines, "space")
    lines_slabs = lines_slabs.transpose(1, 0, 2).reshape(members, spaces * lines_here)
    predicted = (jnp.dot(lines_slabs, pick.T, precision=HIGH) * scale).T

    steps = jnp.array([0, ring - 1, 1, 2], jnp.int32)
    row_y, row_z = me // ring, me % ring
    blocks_at = jnp.concatenate(
        [(row_y ^ side) * ring + (row_z + steps) % ring for side in (0, 1)]
    )
    target = (blocks_at[:, None] * members + jnp.arange(members, dtype=jnp.int32)[None, :]).reshape(1, everyone)
    mix = pl.pallas_call(
        solve_kernel,
        out_shape=jax.ShapeDtypeStruct((members, everyone), jnp.bfloat16),
        scratch_shapes=[
            pltpu.VMEM((everyone, everyone), jnp.float32),
            pltpu.VMEM((2, everyone // 2, everyone // 2), jnp.float32),
        ],
        compiler_params=pltpu.CompilerParams(vmem_limit_bytes=16 * MIB),
        name="solve",
    )(whole, target)
    updated = combine(mix, theta, [own, z_low, z_high, far_a, far_b, y_own, y_low, y_high, y_far_a, y_far_b])
    return (updated, predicted)


def solution(mesh):
    in_specs = (
        P("mem", "space", None, None),
        P("space", None, None),
        P(),
        P("space"),
        P("space", "mem"),
        P("space"),
    )
    out_specs = (P("mem", "space", None, None), P("space", "mem"))
    return jax.shard_map(body, mesh=mesh, in_specs=in_specs, out_specs=out_specs, check_vma=False)
```

time: 451 us -> 284 us (0.63)
  other arithmetic: 111 us -> 5.13 us
  waiting for transfers between devices: 210 us -> 124 us
  Pallas kernels: 0 us -> 69.5 us
  blocking collectives: 58.7 us -> 0 us
  starting transfers between devices: 21.2 us -> 56.5 us
  between operations: 17.3 us -> 0.88 us
  matrix products: 16.3 us -> 4.52 us
  local copies, waits for them, and re-layouts: 15.9 us -> 21.5 us
    psum x1 -> x0, waiting for transfers between devices: 122 us -> none  [body(): gram_part, right_part = lax.psum((gram_part, right_part), 'space')]
    all_to_all x0 -> x5, waiting for transfers between devices: none -> 115 us  [the longest x3 110 us: spread_out(): lax.all_to_all(jnp.broadcast_to(block[None], (count,) + block.shape), axi...]
    pallas_call x0 -> x4, Pallas kernels: none -> 69.5 us  [the longest x1 29.8 us: diffuse(): pl.pallas_call(diffuse_kernel, grid=(members // some,), in_specs=[pl.Bloc...]
    all_gather x2 -> x0, blocking collectives: 58.7 us -> none  [the longest x1 29.9 us: body(): lax.all_gather(noise, 'mem', axis=1, tiled=True)]
    another operation x9 -> x0, other arithmetic: 53.8 us -> none  [the longest x6 34.1 us: body(): factor = jnp.linalg.cholesky(system)]
    ppermute x8 -> x13, waiting for transfers between devices: 45.1 us -> 8.85 us  [the longest x1 8.79 us: body(): start_low = lax.ppermute(start[planes - width:], 'space', forward)]
    reduce_scatter x1 -> x0, waiting for transfers between devices: 35.2 us -> none  [body(): lax.psum_scatter(partial_value, 'space', scatter_dimension=0, tiled=True)]
    all_to_all x0 -> x5, starting transfers between devices: none -> 29.8 us  [the longest x3 14.4 us: spread_out(): lax.all_to_all(jnp.broadcast_to(block[None], (count,) + block.shape), axi...]
  transfers between devices with their start and end apart: 11 -> 18, of which waited for: 11 -> 5; matrix products, arithmetic and copies ran while one was open for 15% -> 6% of each run, Pallas kernels for 0% -> 19%
where the time goes in v1:
time: 284 us; the launch traced here: 282 us
  waiting for transfers between devices  124 us (44%)
  Pallas kernels  69.5 us (24%)
  starting transfers between devices  56.5 us (20%)
  local copies, waits for them, and re-layouts  21.5 us (8%)
  other arithmetic  5.13 us (2%)
  matrix products  4.52 us (2%)
    all_to_all x3, waiting for transfers between devices, spread_out(): lax.all_to_all(jnp.broadcast_to(block[None], (count,) + block.shape), axi...  110 us
    pallas_call x1, Pallas kernels, diffuse(): pl.pallas_call(diffuse_kernel, grid=(members // some,), in_specs=[pl.Bloc...  29.8 us
    pallas_call x1, Pallas kernels, body(): pl.pallas_call(solve_kernel, out_shape=jax.ShapeDtypeStruct((members, eve...  23.5 us
    pallas_call x1, Pallas kernels, combine(): pl.pallas_call(functools.partial(combine_kernel, 1.0 / math.sqrt(everyone...  14.9 us
    all_to_all x3, starting transfers between devices, spread_out(): lax.all_to_all(jnp.broadcast_to(block[None], (count,) + block.shape), axi...  14.4 us
    unnamed x23, local copies, waits for them, and re-layouts  10.8 us
    ppermute x1, waiting for transfers between devices, body(): start_low = lax.ppermute(start[planes - width:], 'space', forward)  8.79 us
    all_to_all x1, starting transfers between devices, body(): by_line = jnp.sum(lax.all_to_all(by_line, 'space', 0, 0), axis=0)  8.48 us
  transfers between devices with their start and end apart: 18, of which 5 were waited for; matrix products, arithmetic and copies ran while one was open for 6% of the time, Pallas kernels for 19%

profile of v1, /device:TPU:1, one launch (start us, length us, event | category | flops | bytes accessed | tf_op | source)
XLA Modules:
  0.0 282.4 jit_solution(7292594642368084605)
XLA Ops:
  0.6 2.7 convert_element_type.10
  3.3 0.9 fusion.14
  4.3 3.3 %collective-permute-start.1 = (bf16[32,3,64,128]{3,2,1,0:T(8,128)(2,1)S(1)}, bf16[32,3,64,128]{3,2,1,0:T(8,128)(2,1)S(1)}, u32[]{:S(2)}, u32[]{:S(2)}) collective-permute-start(bf16[32,3,64,128]{3,2,1,0:T(8,128)(2,1)S(1)} %get-tuple-element.16), channel_id=1, source_target_pairs={{1,0},{2,1},{3,2},{4,3},{5,4},{6,5},{7,6},{8,7},{9,8},{10,9},{11,1... | collective-permute-start | bytes 4718600 | tf_op jit(solution)/shard_map/ppermute | solution.py:252
  7.6 3.1 %collective-permute-start = (bf16[32,3,64,128]{3,2,1,0:T(8,128)(2,1)S(1)}, bf16[32,3,64,128]{3,2,1,0:T(8,128)(2,1)S(1)}, u32[]{:S(2)}, u32[]{:S(2)}) collective-permute-start(bf16[32,3,64,128]{3,2,1,0:T(8,128)(2,1)S(1)} %get-tuple-element.17), channel_id=1, source_target_pairs={{0,1},{1,2},{2,3},{3,4},{4,5},{5,6},{6,7},{7,8},{8,9},{9,10},{10,1... | collective-permute-start | bytes 4718600 | tf_op jit(solution)/shard_map/ppermute | solution.py:251
  10.8 2.4 collective-permute-start.2
  13.2 1.9 collective-permute-start.3
  15.2 1.4 copy.16
  16.5 3.8 %collective-permute-start.5 = (bf16[32,32768]{1,0:T(8,128)(2,1)S(1)}, bf16[32,32768]{1,0:T(8,128)(2,1)}, u32[]{:S(2)}, u32[]{:S(2)}) collective-permute-start(bf16[32,32768]{1,0:T(8,128)(2,1)S(1)} %bitcast.25), channel_id=1, source_target_pairs={{0,48},{16,0},{32,16},{48,32},{64,112},{80,64},{96,80},{112,96},{1... | collective-permute-start | bytes 6291464 | tf_op jit(solution)/shard_map/ppermute | solution.py:263
  20.3 8.8 %collective-permute-done.2 = f32[3,64,128]{2,1,0:T(8,128)S(1)} collective-permute-done((f32[3,64,128]{2,1,0:T(8,128)S(1)}, f32[3,64,128]{2,1,0:T(8,128)S(1)}, u32[]{:S(2)}, u32[]{:S(2)}) %collective-permute-start.2) | collective-permute-done | bytes 98336 | tf_op jit(solution)/shard_map/ppermute | solution.py:253
  29.1 1.6 collective-permute-start.4
  30.8 1.1 copy-done.2
  32.0 1.1 copy-done.4
  33.1 2.9 %collective-permute-start.8 = (bf16[32,32768]{1,0:T(8,128)(2,1)S(1)}, bf16[32,32768]{1,0:T(8,128)(2,1)}, u32[]{:S(2)}, u32[]{:S(2)}) collective-permute-start(bf16[32,32768]{1,0:T(8,128)(2,1)S(1)} %bitcast.27), channel_id=1, source_target_pairs={{0,64},{16,80},{32,96},{48,112},{64,0},{80,16},{96,32},{112,48},{1... | collective-permute-start | bytes 6291464 | tf_op jit(solution)/shard_map/ppermute | solution.py:265
  36.0 0.8 dynamic_slice.3
  36.8 1.7 fusion.1
  38.5 0.9 copy.17
  39.4 8.5 %all-to-all-start.1 = ((f32[16,40,256]{2,1,0:T(8,128)}), f32[16,40,256]{2,1,0:T(8,128)}, u32[]{:S(2)}, u32[]{:S(2)}) async-start(f32[16,40,256]{2,1,0:T(8,128)} %bitcast.23), calls=%async_computation.1 | async-start | bytes 1310720 | tf_op jit(solution)/shard_map/all_to_all | solution.py:275
  48.0 2.2 copy-done
  50.2 1.4 copy-done.3
  51.6 1.4 copy-done.5
  53.0 29.8 %diffuse.1.own_ref = f32[32,256]{1,0:T(8,128)S(1)} custom-call(f32[2]{0:T(128)S(1)} %add_convert_fusion.edge_ref, f32[32,4,64,128]{3,2,1,0:T(8,128)S(1)} %copy-done, bf16[32,3,64,128]{3,2,1,0:T(8,128)(2,1)S(1)} %copy-done.5, bf16[32,3,64,128]{3,2,1,0:T(8,128)(2,1)S(1)} %copy-done.3, f32[10,64,128]{2,1,0:T(8,128)S(1)} %pad_maximum_fusion.start_ref), custom_call_target="tpu_custom_call" | custom-call | flops 314572800 | bytes 8388608 | tf_op jit(solution)/shard_map/diffuse/pallas_call | solution.py:105
  82.9 2.3 slice.23
  85.1 1.8 collective-permute-start.7
  87.0 2.3 slice.22
  89.3 2.7 collective-permute-start.10
  91.9 0.7 broadcast_in_dim.8
  92.7 5.1 %all-to-all-start = ((f32[8,32,256]{2,1,0:T(8,128)}), f32[8,32,256]{2,1,0:T(8,128)S(1)}, u32[]{:S(2)}, u32[]{:S(2)}) async-start(f32[8,32,256]{2,1,0:T(8,128)} %broadcast_in_dim.8), calls=%async_computation | async-start | bytes 524288 | tf_op jit(solution)/shard_map/all_to_all | solution.py:239
  97.7 1.1 reduce_sum.18.data_ref
  98.9 63.6 %all-to-all-done = f32[8,32,256]{2,1,0:T(8,128)S(1)} async-done(((f32[8,32,256]{2,1,0:T(8,128)}), f32[8,32,256]{2,1,0:T(8,128)S(1)}, u32[]{:S(2)}, u32[]{:S(2)}) %all-to-all-start) | async-done | bytes 262176 | tf_op jit(solution)/shard_map/all_to_all | solution.py:239
  162.5 1.2 gram.1
  163.7 6.9 %all-to-all-start.2 = ((f32[16,24,256]{2,1,0:T(8,128)}), f32[16,24,256]{2,1,0:T(8,128)}, u32[]{:S(2)}, u32[]{:S(2)}) async-start(f32[16,24,256]{2,1,0:T(8,128)} %gram.1), calls=%async_computation.2 | async-start | bytes 786432 | tf_op jit(solution)/shard_map/all_to_all | solution.py:288
  170.6 1.3 collective-permute-start.12
  172.0 1.7 collective-permute-start.11
  173.7 5.6 %all-to-all-done.2 = f32[16,24,256]{2,1,0:T(8,128)} async-done(((f32[16,24,256]{2,1,0:T(8,128)}), f32[16,24,256]{2,1,0:T(8,128)}, u32[]{:S(2)}, u32[]{:S(2)}) %all-to-all-start.2) | async-done | bytes 393248 | tf_op jit(solution)/shard_map/all_to_all | solution.py:288
  179.3 0.8 broadcast_in_dim.11
  180.1 4.7 %all-to-all-start.4 = ((f32[16,32,256]{2,1,0:T(8,128)}), f32[16,32,256]{2,1,0:T(8,128)}, u32[]{:S(2)}, u32[]{:S(2)}) async-start(f32[16,32,256]{2,1,0:T(8,128)} %broadcast_in_dim.11), calls=%async_computation.4 | async-start | bytes 1048576 | tf_op jit(solution)/shard_map/all_to_all | solution.py:239
  184.9 0.1 add_multiply_fusion
  184.9 1.0 reduce_sum.19
  186.0 42.1 %all-to-all-done.4 = f32[16,32,256]{2,1,0:T(8,128)} async-done(((f32[16,32,256]{2,1,0:T(8,128)}), f32[16,32,256]{2,1,0:T(8,128)}, u32[]{:S(2)}, u32[]{:S(2)}) %all-to-all-start.4) | async-done | bytes 524320 | tf_op jit(solution)/shard_map/all_to_all | solution.py:239
  228.0 0.8 broadcast_in_dim.10
  228.8 4.6 %all-to-all-start.3 = ((f32[16,24,256]{2,1,0:T(8,128)}), f32[16,24,256]{2,1,0:T(8,128)S(1)}, u32[]{:S(2)}, u32[]{:S(2)}) async-start(f32[16,24,256]{2,1,0:T(8,128)} %broadcast_in_dim.10), calls=%async_computation.3 | async-start | bytes 786432 | tf_op jit(solution)/shard_map/all_to_all | solution.py:239
  233.5 0.1 add.84.target_ref
  233.6 1.1 copy.12
  234.7 2.8 fusion.4
  237.5 4.2 %all-to-all-done.3.parts_ref = f32[16,24,256]{2,1,0:T(8,128)S(1)} async-done(((f32[16,24,256]{2,1,0:T(8,128)}), f32[16,24,256]{2,1,0:T(8,128)S(1)}, u32[]{:S(2)}, u32[]{:S(2)}) %all-to-all-start.3) | async-done | bytes 393248 | tf_op jit(solution)/shard_map/all_to_all | solution.py:239
  241.7 23.5 %solve.1.mix_ref = bf16[32,256]{1,0:T(8,128)(2,1)S(1)} custom-call(f32[16,24,256]{2,1,0:T(8,128)S(1)} %all-to-all-done.3.parts_ref, s32[1,256]{1,0:T(1,128)S(1)} %add.84.target_ref), custom_call_target="tpu_custom_call" | custom-call | tf_op jit(solution)/shard_map/solve/pallas_call | solution.py:310
  265.3 2.2 copy-done.1
  267.5 14.9 %combine.1 = f32[32,256,128]{2,1,0:T(8,128)} custom-call(bf16[32,256]{1,0:T(8,128)(2,1)S(1)} %solve.1.mix_ref, f32[32,256,128]{2,1,0:T(8,128)S(1)} %bitcast.24, bf16[32,32768]{1,0:T(8,128)(2,1)S(1)} %bitcast.28, bf16[32,32768]{1,0:T(8,128)(2,1)} %collective-permute-done.4.refs_1_, bf16[32,32768]{1,0:T(8,128)(2,1)} %collective-permute-done.5.refs_2_, ...), custom_call_target="tpu_custom_call" | custom-call | flops 536870912 | bytes 25165824 | tf_op jit(solution)/shard_map/combine/pallas_call | solution.py:220
  (39 shorter events, 0.3 us)
Async XLA Ops:
  3.3 7.4 %copy-start.6 = (f32[4,64,128]{2,1,0:T(8,128)S(1)}, f32[4,64,128]{2,1,0:T(8,128)}, u32[]{:S(2)}) copy-start(f32[4,64,128]{2,1,0:T(8,128)} %param.8) | copy-start | bytes 393220
  4.3 26.5 %collective-permute-start.1 = (bf16[32,3,64,128]{3,2,1,0:T(8,128)(2,1)S(1)}, bf16[32,3,64,128]{3,2,1,0:T(8,128)(2,1)S(1)}, u32[]{:S(2)}, u32[]{:S(2)}) collective-permute-start(bf16[32,3,64,128]{3,2,1,0:T(8,128)(2,1)S(1)} %get-tuple-element.16), channel_id=1, source_target_pairs={{1,0},{2,1},{3,2},{4,3},{5,4},{6,5},{7,6},{8,7},{9,8},{10,9},{11,1... | collective-permute-start | bytes 4718600 | tf_op jit(solution)/shard_map/ppermute | solution.py:252
  7.6 24.3 %collective-permute-start = (bf16[32,3,64,128]{3,2,1,0:T(8,128)(2,1)S(1)}, bf16[32,3,64,128]{3,2,1,0:T(8,128)(2,1)S(1)}, u32[]{:S(2)}, u32[]{:S(2)}) collective-permute-start(bf16[32,3,64,128]{3,2,1,0:T(8,128)(2,1)S(1)} %get-tuple-element.17), channel_id=1, source_target_pairs={{0,1},{1,2},{2,3},{3,4},{4,5},{5,6},{6,7},{7,8},{8,9},{9,10},{10,1... | collective-permute-start | bytes 4718600 | tf_op jit(solution)/shard_map/ppermute | solution.py:251
  10.8 18.4 %collective-permute-start.2 = (f32[3,64,128]{2,1,0:T(8,128)S(1)}, f32[3,64,128]{2,1,0:T(8,128)S(1)}, u32[]{:S(2)}, u32[]{:S(2)}) collective-permute-start(f32[3,64,128]{2,1,0:T(8,128)S(1)} %get-tuple-element.18), channel_id=1, source_target_pairs={{0,1},{1,2},{2,3},{3,4},{4,5},{5,6},{6,7},{7,8},{8,9},{9,10},{10,1... | collective-permute-start | bytes 294920 | tf_op jit(solution)/shard_map/ppermute | solution.py:253
  13.2 17.6 %collective-permute-start.3 = (f32[3,64,128]{2,1,0:T(8,128)S(1)}, f32[3,64,128]{2,1,0:T(8,128)S(1)}, u32[]{:S(2)}, u32[]{:S(2)}) collective-permute-start(f32[3,64,128]{2,1,0:T(8,128)S(1)} %get-tuple-element.19), channel_id=1, source_target_pairs={{1,0},{2,1},{3,2},{4,3},{5,4},{6,5},{7,6},{8,7},{9,8},{10,9},{11,1... | collective-permute-start | bytes 294920 | tf_op jit(solution)/shard_map/ppermute | solution.py:254
  15.1 21.7 %copy-start.9 = (f32[256]{0:T(256)S(1)}, f32[256]{0:T(256)}, u32[]{:S(2)}) copy-start(f32[256]{0:T(256)} %param.12) | copy-start | bytes 3076
  15.1 21.7 %copy-start.7 = (f32[256,32]{0,1:T(8,128)S(1)}, f32[256,32]{0,1:T(8,128)}, u32[]{:S(2)}) copy-start(f32[256,32]{0,1:T(8,128)} %param.11) | copy-start | bytes 98308
  15.1 21.6 %copy-start.8 = (f32[256]{0:T(256)S(1)}, f32[256]{0:T(256)}, u32[]{:S(2)}) copy-start(f32[256]{0:T(256)} %param.10) | copy-start | bytes 3076
  16.5 66.3 %collective-permute-start.5 = (bf16[32,32768]{1,0:T(8,128)(2,1)S(1)}, bf16[32,32768]{1,0:T(8,128)(2,1)}, u32[]{:S(2)}, u32[]{:S(2)}) collective-permute-start(bf16[32,32768]{1,0:T(8,128)(2,1)S(1)} %bitcast.25), channel_id=1, source_target_pairs={{0,48},{16,0},{32,16},{48,32},{64,112},{80,64},{96,80},{112,96},{1... | collective-permute-start | bytes 6291464 | tf_op jit(solution)/shard_map/ppermute | solution.py:263
  29.1 53.7 %collective-permute-start.4 = (bf16[32,32768]{1,0:T(8,128)(2,1)S(1)}, bf16[32,32768]{1,0:T(8,128)(2,1)}, u32[]{:S(2)}, u32[]{:S(2)}) collective-permute-start(bf16[32,32768]{1,0:T(8,128)(2,1)S(1)} %bitcast.26), channel_id=1, source_target_pairs={{0,16},{16,32},{32,48},{48,0},{64,80},{80,96},{96,112},{112,64},{1... | collective-permute-start | bytes 6291464 | tf_op jit(solution)/shard_map/ppermute | solution.py:262
  30.8 1.1 copy-start.2
  32.0 1.1 copy-start.4
  33.1 56.1 %collective-permute-start.8 = (bf16[32,32768]{1,0:T(8,128)(2,1)S(1)}, bf16[32,32768]{1,0:T(8,128)(2,1)}, u32[]{:S(2)}, u32[]{:S(2)}) collective-permute-start(bf16[32,32768]{1,0:T(8,128)(2,1)S(1)} %bitcast.27), channel_id=1, source_target_pairs={{0,64},{16,80},{32,96},{48,112},{64,0},{80,16},{96,32},{112,48},{1... | collective-permute-start | bytes 6291464 | tf_op jit(solution)/shard_map/ppermute | solution.py:265
  39.4 52.5 %all-to-all-start.1 = ((f32[16,40,256]{2,1,0:T(8,128)}), f32[16,40,256]{2,1,0:T(8,128)}, u32[]{:S(2)}, u32[]{:S(2)}) async-start(f32[16,40,256]{2,1,0:T(8,128)} %bitcast.23), calls=%async_computation.1 | async-start | bytes 1310720 | tf_op jit(solution)/shard_map/all_to_all | solution.py:275
  48.0 2.2 copy-start
  50.2 1.4 copy-start.3
  51.6 1.4 copy-start.5
  85.1 85.5 %collective-permute-start.7 = (bf16[16,32768]{1,0:T(8,128)(2,1)}, bf16[16,32768]{1,0:T(8,128)(2,1)S(1)}, u32[]{:S(2)}, u32[]{:S(2)}) collective-permute-start(bf16[16,32768]{1,0:T(8,128)(2,1)} %slice.23), channel_id=1, source_target_pairs={{0,48},{16,0},{32,16},{48,32},{64,112},{80,64},{96,80},{112,96},{1... | collective-permute-start | bytes 3145736 | tf_op jit(solution)/shard_map/ppermute | solution.py:294
  89.2 82.7 %collective-permute-start.6 = (bf16[16,32768]{1,0:T(8,128)(2,1)}, bf16[16,32768]{1,0:T(8,128)(2,1)}, u32[]{:S(2)}, u32[]{:S(2)}) collective-permute-start(bf16[16,32768]{1,0:T(8,128)(2,1)} %slice.22), channel_id=1, source_target_pairs={{0,16},{16,32},{32,48},{48,0},{64,80},{80,96},{96,112},{112,64},{1... | collective-permute-start | bytes 3145736 | tf_op jit(solution)/shard_map/ppermute | solution.py:293
  89.3 176.0 %collective-permute-start.10 = (bf16[32,32768]{1,0:T(8,128)(2,1)}, bf16[32,32768]{1,0:T(8,128)(2,1)}, u32[]{:S(2)}, u32[]{:S(2)}) collective-permute-start(bf16[32,32768]{1,0:T(8,128)(2,1)} %collective-permute-done.8.refs_5_), channel_id=1, source_target_pairs={{0,48},{16,0},{32,16},{48,32},{64,112},{80,64},{96,80},{112,96},{1... | collective-permute-start | bytes 6291464 | tf_op jit(solution)/shard_map/ppermute | solution.py:296
  91.9 173.3 %collective-permute-start.9 = (bf16[32,32768]{1,0:T(8,128)(2,1)}, bf16[32,32768]{1,0:T(8,128)(2,1)}, u32[]{:S(2)}, u32[]{:S(2)}) collective-permute-start(bf16[32,32768]{1,0:T(8,128)(2,1)} %collective-permute-done.8.refs_5_), channel_id=1, source_target_pairs={{0,16},{16,32},{32,48},{48,0},{64,80},{80,96},{96,112},{112,64},{1... | collective-permute-start | bytes 6291464 | tf_op jit(solution)/shard_map/ppermute | solution.py:295
  92.7 92.2 %copy-start.10 = (s32[4]{0:T(128)S(1)}, s32[4]{0:T(128)}, u32[]{:S(2)}) copy-start(s32[4]{0:T(128)} %constant.65.clone) | copy-start | bytes 52
  92.7 69.8 %all-to-all-start = ((f32[8,32,256]{2,1,0:T(8,128)}), f32[8,32,256]{2,1,0:T(8,128)S(1)}, u32[]{:S(2)}, u32[]{:S(2)}) async-start(f32[8,32,256]{2,1,0:T(8,128)} %broadcast_in_dim.8), calls=%async_computation | async-start | bytes 524288 | tf_op jit(solution)/shard_map/all_to_all | solution.py:239
  163.7 15.6 %all-to-all-start.2 = ((f32[16,24,256]{2,1,0:T(8,128)}), f32[16,24,256]{2,1,0:T(8,128)}, u32[]{:S(2)}, u32[]{:S(2)}) async-start(f32[16,24,256]{2,1,0:T(8,128)} %gram.1), calls=%async_computation.2 | async-start | bytes 786432 | tf_op jit(solution)/shard_map/all_to_all | solution.py:288
  170.6 94.6 %collective-permute-start.12 = (bf16[16,32768]{1,0:T(8,128)(2,1)S(1)}, bf16[16,32768]{1,0:T(8,128)(2,1)}, u32[]{:S(2)}, u32[]{:S(2)}) collective-permute-start(bf16[16,32768]{1,0:T(8,128)(2,1)S(1)} %collective-permute-done.7.refs_4_), channel_id=1, source_target_pairs={{0,64},{16,80},{32,96},{48,112},{64,0},{80,16},{96,32},{112,48},{1... | collective-permute-start | bytes 3145736 | tf_op jit(solution)/shard_map/ppermute | solution.py:298
  172.0 93.3 %collective-permute-start.11 = (bf16[16,32768]{1,0:T(8,128)(2,1)}, bf16[16,32768]{1,0:T(8,128)(2,1)}, u32[]{:S(2)}, u32[]{:S(2)}) collective-permute-start(bf16[16,32768]{1,0:T(8,128)(2,1)} %collective-permute-done.6.refs_3_), channel_id=1, source_target_pairs={{0,64},{16,80},{32,96},{48,112},{64,0},{80,16},{96,32},{112,48},{1... | collective-permute-start | bytes 3145736 | tf_op jit(solution)/shard_map/ppermute | solution.py:297
  180.1 47.9 %all-to-all-start.4 = ((f32[16,32,256]{2,1,0:T(8,128)}), f32[16,32,256]{2,1,0:T(8,128)}, u32[]{:S(2)}, u32[]{:S(2)}) async-start(f32[16,32,256]{2,1,0:T(8,128)} %broadcast_in_dim.11), calls=%async_computation.4 | async-start | bytes 1048576 | tf_op jit(solution)/shard_map/all_to_all | solution.py:239
  228.8 12.9 %all-to-all-start.3 = ((f32[16,24,256]{2,1,0:T(8,128)}), f32[16,24,256]{2,1,0:T(8,128)S(1)}, u32[]{:S(2)}, u32[]{:S(2)}) async-start(f32[16,24,256]{2,1,0:T(8,128)} %broadcast_in_dim.10), calls=%async_computation.3 | async-start | bytes 786432 | tf_op jit(solution)/shard_map/all_to_all | solution.py:239
  265.3 2.2 copy-start.1

commit v2 on v1

v2 whole, which is shorter than its diff:
```python
import functools
import math

import jax
import jax.numpy as jnp
from jax import lax
from jax.experimental import pallas as pl
from jax.experimental.pallas import tpu as pltpu
from jax.sharding import PartitionSpec as P

STEPS = 3
STEP_SIZE = 0.055
OUTSIDE = 1.0 / (2.0 * STEP_SIZE)
HIGH = lax.Precision.HIGHEST
NT = (((1,), (1,)), ((), ()))
MIB = 1 << 20
PIVOTS = 8


def inverse(x):
    return pl.reciprocal(x, approx=True)


def diffuse_kernel(
    edge_ref, theta_ref, low_ref, high_ref, low_start_ref, high_start_ref, own_start_ref,
    out_ref, cx, cy, cz, keep, u0, u1, u2, u3,
):
    members, planes, rows, lanes = theta_ref.shape
    width = low_ref.shape[1]
    total = planes + 2 * width
    row_at = lax.broadcasted_iota(jnp.int32, (rows, lanes), 0)
    lane_at = lax.broadcasted_iota(jnp.int32, (rows, lanes), 1)
    last_row, last_lane = row_at == rows - 1, lane_at == lanes - 1
    sides = (
        (row_at == 0).astype(jnp.float32)
        + last_row.astype(jnp.float32)
        + (lane_at == 0).astype(jnp.float32)
        + last_lane.astype(jnp.float32)
    )
    low_edge, high_edge = edge_ref[0], edge_ref[1]

    @pl.when(pl.program_id(0) == 0)
    def _():
        u0[0:width] = low_start_ref[0].astype(jnp.float32) + low_start_ref[1].astype(jnp.float32)
        u0[width : width + planes] = own_start_ref[...]
        u0[width + planes :] = high_start_ref[0].astype(jnp.float32) + high_start_ref[1].astype(jnp.float32)

    def up(v, axis):
        return pltpu.roll(v, v.shape[axis] - 1, axis)

    def down(v, axis):
        return pltpu.roll(v, 1, axis)

    @pl.loop(0, members)
    def _(m):
        def resistance(p):
            if p < width:
                t = low_ref[m, p].astype(jnp.float32)
            elif p < width + planes:
                t = theta_ref[m, p - width]
            else:
                t = high_ref[m, p - width - planes].astype(jnp.float32)
            return jnp.exp(math.log(OUTSIDE) - t)

        fields = [u0, u1, u2, u3]
        flux_z = [None] * STEPS

        def advance(step, p):
            source = fields[step]
            u = source[p]
            if flux_z[step] is None:
                flux_z[step] = cz[p - 1] * (u - source[p - 1])
            fx = cx[p] * (up(u, 0) - u)
            fy = cy[p] * (up(u, 1) - u)
            fz = cz[p] * (source[p + 1] - u)
            new = keep[p] * u + ((fx - down(fx, 0)) + (fy - down(fy, 1)) + (fz - flux_z[step]))
            flux_z[step] = fz
            if p < width:
                new = new * low_edge
            elif p >= width + planes:
                new = new * high_edge
            if step == STEPS - 1:
                u3[p - width] = new
            else:
                fields[step + 1][p] = new

        before = None
        for p in range(total):
            r = resistance(p)
            if before is not None:
                cz[p - 1] = inverse(before + r)
            before = r
            if 1 <= p < total - 1:
                cx[p] = jnp.where(last_row, 0.0, inverse(r + up(r, 0)))
                cy[p] = jnp.where(last_lane, 0.0, inverse(r + up(r, 1)))
                keep[p] = 1.0 - sides * inverse(r + OUTSIDE)
            for step in range(STEPS):
                q = p - 1 - step
                if step + 1 <= q < total - 1 - step:
                    advance(step, q)
        ones = jnp.ones((8, lanes), jnp.float32)
        sums = lax.dot_general(
            ones, u3[...].reshape(planes * rows, lanes), NT, precision=HIGH, preferred_element_type=jnp.float32
        )
        out_ref[pl.ds(m, 1), :] = sums[0:1]


def diffuse(theta, first, low, high, begin_low, begin_high, start, edges):
    planes, rows, lanes = theta.shape[1:]
    members, width = low.shape[:2]
    members -= members % 8
    total = planes + 2 * width
    some = 8
    skip, last = first // some, begin_low.shape[0] // 2 - 1
    shape = (total, rows, lanes)
    return pl.pallas_call(
        diffuse_kernel,
        grid=(members // some,),
        in_specs=[
            pl.BlockSpec(memory_space=pltpu.SMEM),
            pl.BlockSpec((some, planes, rows, lanes), lambda i: (i + skip, 0, 0, 0)),
            pl.BlockSpec((some, width, rows, lanes), lambda i: (i, 0, 0, 0)),
            pl.BlockSpec((some, width, rows, lanes), lambda i: (i, 0, 0, 0)),
            pl.BlockSpec((2, width, rows, lanes), lambda i: (last, 0, 0, 0)),
            pl.BlockSpec((2, width, rows, lanes), lambda i: (last, 0, 0, 0)),
            pl.BlockSpec((planes, rows, lanes), lambda i: (0, 0, 0)),
        ],
        out_specs=pl.BlockSpec((some, planes * rows), lambda i: (i, 0)),
        out_shape=jax.ShapeDtypeStruct((members, planes * rows), jnp.float32),
        scratch_shapes=[pltpu.VMEM(shape, jnp.float32)] * 7 + [pltpu.VMEM((planes, rows, lanes), jnp.float32)],
        compiler_params=pltpu.CompilerParams(vmem_limit_bytes=50 * MIB),
        cost_estimate=pl.CostEstimate(flops=300 * theta.size, bytes_accessed=50 * theta.size, transcendentals=12 * theta.size),
        name="diffuse",
    )(edges, theta, low, high, begin_low, begin_high, start)


def gram_kernel(scale, lines_ref, data_ref, weight_ref, out_ref):
    everyone, count = lines_ref.shape
    value = lines_ref[...] * scale
    dev = value - jnp.mean(value, axis=0, keepdims=True)
    weight = weight_ref[0:1, :]
    dot = functools.partial(lax.dot_general, dimension_numbers=NT, precision=HIGH, preferred_element_type=jnp.float32)
    gram = dot(dev * (weight * (1.0 / (everyone - 1))), dev)
    right = dot((data_ref[...] - weight * value) * (1.0 / math.sqrt(everyone - 1)), dev)
    chunks = out_ref.shape[0]
    a = everyone // chunks
    for c in range(chunks):
        out_ref[c, 0:a] = gram[a * c : a * (c + 1)]
        out_ref[c, a:] = right[a * c : a * (c + 1)]


def invert_block(block):
    size = block.shape[0]
    lane_at = lax.broadcasted_iota(jnp.int32, (1, size), 1)
    row_at = lax.broadcasted_iota(jnp.int32, (8, 1), 0)
    groups = [block[8 * g : 8 * g + 8] for g in range(size // 8)]
    span = range(PIVOTS)
    for k in range(0, size, PIVOTS):
        g, s = divmod(k, 8)
        here = (lane_at >= k) & (lane_at < k + PIVOTS)
        rows = [groups[g][s + i : s + i + 1] for i in span]
        pivot = [[jnp.broadcast_to(row[:, k + j : k + j + 1], (1, size)) for j in span] for row in rows]
        rows = [jnp.where(here, (lane_at == k + i).astype(jnp.float32), row) for i, row in enumerate(rows)]
        for i in span:
            d = inverse(pivot[i][i])
            rows[i] = rows[i] * d
            for j in range(i + 1, PIVOTS):
                pivot[i][j] = pivot[i][j] * d
            for other in span:
                if other != i:
                    f = pivot[other][i]
                    rows[other] = rows[other] - f * rows[i]
                    for j in range(i + 1, PIVOTS):
                        pivot[other][j] = pivot[other][j] - f * pivot[i][j]
        new = []
        for i, old in enumerate(groups):
            next_rows = jnp.where(here, 0.0, old)
            for j in span:
                next_rows = next_rows - old[:, k + j : k + j + 1] * rows[j]
            if i == g:
                for j in span:
                    next_rows = jnp.where(row_at == s + j, rows[j], next_rows)
            new.append(next_rows)
        groups = new
    return jnp.concatenate(groups, axis=0)


def solve_kernel(parts_ref, out_ref, work, rhs, inv):
    chunks, depth, size = parts_ref.shape
    a = size // chunks
    half = size // 2
    for c in range(chunks):
        work[a * c : a * (c + 1)] = parts_ref[c, 0:a]
        rhs[a * c : a * (c + 1)] = parts_ref[c, a:]
    eye = (
        lax.broadcasted_iota(jnp.int32, (half, half), 0) == lax.broadcasted_iota(jnp.int32, (half, half), 1)
    ).astype(jnp.float32)
    work[0:half, 0:half] += eye
    work[half:, half:] += eye
    dot = functools.partial(jnp.dot, precision=HIGH, preferred_element_type=jnp.float32)

    @pl.loop(0, 2)
    def _(i):
        at = pl.ds(pl.multiple_of(i * half, half), half)

        @pl.when(i == 1)
        def _():
            cross = dot(work[half:, 0:half], inv[0])
            work[half:, half:] = work[half:, half:] - dot(cross, work[0:half, half:])

        inv[i] = invert_block(work[at, at])

    cross = dot(work[half:, 0:half], inv[0])
    first = dot(rhs[:, 0:half], inv[0])
    second = dot(rhs[:, half:] - dot(first, work[0:half, half:]), inv[1])
    out_ref[:, 0:half] = (first - dot(second, cross)).astype(jnp.bfloat16)
    out_ref[:, half:] = second.astype(jnp.bfloat16)


def shared_kernel(scale, mix_ref, fields_ref, out_ref):
    some = 512
    for c in range(0, out_ref.shape[1], some):
        result = jnp.dot(mix_ref[...], fields_ref[:, c : c + some], preferred_element_type=jnp.float32)
        out_ref[:, c : c + some] = (result * scale).astype(jnp.bfloat16)


def finish_kernel(theta_ref, change_ref, out_ref):
    members, some, lanes = theta_ref.shape
    for m in range(0, members, 8):
        change = change_ref[0, m : m + 8, :].astype(jnp.float32)
        change = jnp.stack([change[:, r * lanes : (r + 1) * lanes] for r in range(some)])
        out_ref[m : m + 8] = theta_ref[m : m + 8] + jnp.swapaxes(change, 0, 1)


def finish(theta, changes):
    members, rows, lanes = theta.shape
    chunks, _, cells = changes.shape
    some = cells // lanes
    block = pl.BlockSpec((members, some, lanes), lambda i: (0, i, 0))
    return pl.pallas_call(
        finish_kernel,
        grid=(chunks,),
        in_specs=[block, pl.BlockSpec((1, members, cells), lambda i: (i, 0, 0))],
        out_specs=block,
        out_shape=jax.ShapeDtypeStruct(theta.shape, jnp.float32),
        compiler_params=pltpu.CompilerParams(vmem_limit_bytes=50 * MIB),
        cost_estimate=pl.CostEstimate(flops=2 * changes.size, bytes_accessed=10 * changes.size, transcendentals=0),
        name="finish",
    )(theta, changes)


def after(block, *others):
    return lax.optimization_barrier((block,) + others)[0]


def spread_out(block, axis):
    count = lax.axis_size(axis)
    return lax.all_to_all(jnp.broadcast_to(block[None], (count,) + block.shape), axis, 0, 0)


def after(block, *others):
    return lax.optimization_barrier((block,) + others)[0]


def body(theta, start, sensors, observed, noise, variance):
    members, planes, rows, lanes = theta.shape
    spaces, mems = lax.axis_size("space"), lax.axis_size("mem")
    lines_here = planes * rows
    everyone = members * mems
    mine, me = lax.axis_index("space"), lax.axis_index("mem")
    width = STEPS
    scale = 1.0 / math.sqrt(lanes)
    line_at = jnp.arange(spaces * lines_here, dtype=jnp.int32)
    rows_here = observed.shape[0]
    sensors_here = lax.dynamic_slice_in_dim(sensors, mine * rows_here, rows_here, 0)
    pick = (sensors_here[:, None] == line_at[None, :]).astype(jnp.float32)
    inv_var = 1.0 / variance
    data = jnp.concatenate([(observed[None, :] + noise.T) * inv_var[None, :], inv_var[None, :]], axis=0)
    data = jnp.pad(data, ((0, 7), (0, 0)))
    by_line = jnp.dot(data, pick, precision=HIGH).reshape(members + 8, spaces, lines_here).transpose(1, 0, 2)
    by_line = lax.all_to_all(by_line, "space", 0, 0)
    low_theta = theta.astype(jnp.bfloat16)
    coarse = lax.reduce_precision(start, 8, 7)
    fine = (start - coarse).astype(jnp.bfloat16)
    begin = jnp.stack([coarse.astype(jnp.bfloat16), fine])
    forward = [(i, i + 1) for i in range(spaces - 1)]
    backward = [(i + 1, i) for i in range(spaces - 1)]
    half = members // 2
    top, bottom = slice(planes - width, planes), slice(0, width)
    to_high = jnp.concatenate([low_theta[:half, top], begin[:, top]], axis=0)
    to_low = jnp.concatenate([low_theta[:half, bottom], begin[:, bottom]], axis=0)
    to_high_b, to_low_b = low_theta[half:, top], low_theta[half:, bottom]
    share_rows = lines_here // mems
    shares = low_theta.reshape(members, mems, share_rows, lanes).transpose(1, 0, 2, 3)
    shares = after(shares, by_line, to_high, to_low, to_high_b, to_low_b)
    halo_low = lax.ppermute(to_high, "space", forward)
    halo_high = lax.ppermute(to_low, "space", backward)
    halo_low_b = lax.ppermute(to_high_b, "space", forward)
    halo_high_b = lax.ppermute(to_low_b, "space", backward)
    edges = jnp.stack([mine > 0, mine < spaces - 1]).astype(jnp.float32)

    shared = lax.all_to_all(shares, "mem", 0, 0)
    cells = share_rows * lanes

    lines_a = diffuse(theta, 0, halo_low, halo_high, halo_low, halo_high, start, edges)
    lines_b = diffuse(theta, half, halo_low_b, halo_high_b, halo_low, halo_high, start, after(edges, lines_a))
    lines = jnp.concatenate([lines_a, lines_b], axis=0)
    lines, shared = lax.optimization_barrier((lines, shared))
    by_line = jnp.sum(by_line, axis=0)
    weights = by_line[members:]
    both = spread_out(jnp.stack([lines, by_line[:members]]), "mem")
    both, shared = lax.optimization_barrier((both, shared.reshape(everyone, cells)))
    lines_all = both[:, 0].reshape(everyone, lines_here)
    data_all = both[:, 1].reshape(everyone, lines_here)
    partial_sums = pl.pallas_call(
        functools.partial(gram_kernel, scale),
        out_shape=jax.ShapeDtypeStruct((spaces, 2 * everyone // spaces, everyone), jnp.float32),
        compiler_params=pltpu.CompilerParams(vmem_limit_bytes=50 * MIB),
        name="gram",
    )(lines_all, data_all, weights)
    sums = jnp.sum(lax.all_to_all(partial_sums, "space", 0, 0), axis=0)
    whole = spread_out(sums, "space")

    lines_slabs = spread_out(after(lines, whole), "space")
    lines_slabs = lines_slabs.transpose(1, 0, 2).reshape(members, spaces * lines_here)
    predicted = (jnp.dot(lines_slabs, pick.T, precision=HIGH) * scale).T

    mix = pl.pallas_call(
        solve_kernel,
        out_shape=jax.ShapeDtypeStruct((everyone, everyone), jnp.bfloat16),
        scratch_shapes=[
            pltpu.VMEM((everyone, everyone), jnp.float32),
            pltpu.VMEM((everyone, everyone), jnp.float32),
            pltpu.VMEM((2, everyone // 2, everyone // 2), jnp.float32),
        ],
        compiler_params=pltpu.CompilerParams(vmem_limit_bytes=16 * MIB),
        cost_estimate=pl.CostEstimate(flops=1 << 30, bytes_accessed=30 * MIB, transcendentals=0),
        name="solve",
    )(whole)
    factor = 1.0 / math.sqrt(everyone - 1)
    changes = pl.pallas_call(
        functools.partial(shared_kernel, factor),
        out_shape=jax.ShapeDtypeStruct((everyone, cells), jnp.bfloat16),
        compiler_params=pltpu.CompilerParams(vmem_limit_bytes=50 * MIB),
        name="shared",
    )(mix, shared)
    changes = lax.all_to_all(changes.reshape(mems, members, cells), "mem", 0, 0)
    updated = finish(theta.reshape(members, lines_here, lanes), changes).reshape(theta.shape)
    return (updated, predicted)


def solution(mesh):
    in_specs = (
        P("mem", "space", None, None),
        P("space", None, None),
        P(),
        P("space"),
        P("space", "mem"),
        P("space"),
    )
    out_specs = (P("mem", "space", None, None), P("space", "mem"))
    return jax.shard_map(body, mesh=mesh, in_specs=in_specs, out_specs=out_specs, check_vma=False)
```

time: 284 us -> 181 us (0.64)
  waiting for transfers between devices: 124 us -> 37.8 us
  blocking collectives: 0 us -> 29.7 us
  Pallas kernels: 69.5 us -> 47.7 us
  starting transfers between devices: 56.5 us -> 38.9 us
  local copies, waits for them, and re-layouts: 21.5 us -> 13.1 us
    all_to_all x3 -> x2, waiting for transfers between devices: 110 us -> 5.79 us  [spread_out(): lax.all_to_all(jnp.broadcast_to(block[None], (count,) + block.shape), axi...]
    all_to_all x0 -> x2, blocking collectives: none -> 29.7 us  [the longest x1 16.2 us: body(): sums = jnp.sum(lax.all_to_all(partial_sums, 'space', 0, 0), axis=0)]
    all_to_all x2 -> x3, waiting for transfers between devices: 5.62 us -> 26.4 us  [the longest x1 23.3 us: body(): changes = lax.all_to_all(changes.reshape(mems, members, cells), 'mem', 0, 0)]
    pallas_call x2 -> x3, Pallas kernels: 38.4 us -> 18.8 us  [the longest x1 9.53 us: body(): pl.pallas_call(solve_kernel, out_shape=jax.ShapeDtypeStruct((everyone, ev...]
    ppermute x13 -> x4, starting transfers between devices: 26.7 us -> 10 us  [the longest x1 3.64 us: body(): halo_low_b = lax.ppermute(to_high_b, 'space', forward)]
    unnamed x23 -> x7, local copies, waits for them, and re-layouts: 10.8 us -> 6.06 us
    slice x4 -> x3, local copies, waits for them, and re-layouts: 5.51 us -> 1.82 us  [the longest x1 1.78 us: body(): to_high_b, to_low_b = (low_theta[half:, top], low_theta[half:, bottom])]
    all_to_all x3 -> x2, starting transfers between devices: 14.4 us -> 11.1 us  [spread_out(): lax.all_to_all(jnp.broadcast_to(block[None], (count,) + block.shape), axi...]
  transfers between devices with their start and end apart: 18 -> 9, of which waited for: 5 -> 5; matrix products, arithmetic and copies ran while one was open for 6% -> 9% of each run, Pallas kernels for 19% -> 22%
where the time goes in v2:
time: 181 us; the launch traced here: 180 us
  Pallas kernels  47.7 us (26%)
  starting transfers between devices  38.9 us (21%)
  waiting for transfers between devices  37.8 us (21%)
  blocking collectives  29.7 us (16%)
  local copies, waits for them, and re-layouts  13.1 us (7%)
  other arithmetic  7.45 us (4%)
  matrix products  4.52 us (2%)
    pallas_call x2, Pallas kernels, diffuse(): pl.pallas_call(diffuse_kernel, grid=(members // some,), in_specs=[pl.Bloc...  28.1 us
    all_to_all x1, waiting for transfers between devices, body(): changes = lax.all_to_all(changes.reshape(mems, members, cells), 'mem', 0, 0)  23.3 us
    all_to_all x1, blocking collectives, body(): sums = jnp.sum(lax.all_to_all(partial_sums, 'space', 0, 0), axis=0)  16.2 us
    all_to_all x1, blocking collectives, spread_out(): lax.all_to_all(jnp.broadcast_to(block[None], (count,) + block.shape), axi...  13.5 us
    all_to_all x2, starting transfers between devices, spread_out(): lax.all_to_all(jnp.broadcast_to(block[None], (count,) + block.shape), axi...  11.1 us
    pallas_call x1, Pallas kernels, body(): pl.pallas_call(solve_kernel, out_shape=jax.ShapeDtypeStruct((everyone, ev...  9.53 us
    all_to_all x1, starting transfers between devices, body(): shared = lax.all_to_all(shares, 'mem', 0, 0)  7.37 us
    pallas_call x1, Pallas kernels, finish(): pl.pallas_call(finish_kernel, grid=(chunks,), in_specs=[block, pl.BlockSp...  6.99 us
  transfers between devices with their start and end apart: 9, of which 5 were waited for; matrix products, arithmetic and copies ran while one was open for 9% of the time, Pallas kernels for 22%

profile of v2, /device:TPU:1, one launch (start us, length us, event | category | flops | bytes accessed | tf_op | source)
XLA Modules:
  0.0 180.0 jit_solution(3701896318803568355)
XLA Ops:
  0.6 0.0 copy-start.1
  0.6 0.7 broadcast_divide_fusion
  1.4 0.8 dynamic_slice.3
  2.1 0.8 multiply_bitcast_fusion
  2.9 1.7 fusion.1
  4.6 0.9 copy.21
  5.5 6.8 %all-to-all-start = ((f32[16,40,256]{2,1,0:T(8,128)}), f32[16,40,256]{2,1,0:T(8,128)S(1)}, u32[]{:S(2)}, u32[]{:S(2)}) async-start(f32[16,40,256]{2,1,0:T(8,128)} %bitcast.36), calls=%async_computation | async-start | bytes 1310720 | tf_op jit(solution)/shard_map/all_to_all | solution.py:281
  12.3 0.0 copy-done.1
  12.4 2.7 %convert_element_type.16 = bf16[32,4,64,128]{3,2,1,0:T(8,128)(2,1)S(1)} convert(f32[32,4,64,128]{3,2,1,0:T(8,128)} %theta_ref.3) | non-fusion elementwise | flops 1048576 | bytes 6291456 | tf_op jit(solution)/shard_map/convert_element_type | solution.py:282
  15.1 1.8 copy.20
  16.8 1.8 fusion.18
  18.6 1.0 fusion.5
  19.6 1.0 pad_maximum_fusion.1
  20.6 3.1 %all-to-all-done = f32[16,40,256]{2,1,0:T(8,128)S(1)} async-done(((f32[16,40,256]{2,1,0:T(8,128)}), f32[16,40,256]{2,1,0:T(8,128)S(1)}, u32[]{:S(2)}, u32[]{:S(2)}) %all-to-all-start) | async-done | bytes 655392 | tf_op jit(solution)/shard_map/all_to_all | solution.py:281
  23.7 0.0 copy-start.2
  23.7 0.8 copy-done.2
  24.6 7.4 %all-to-all-start.1 = ((bf16[8,32,32,128]{3,2,1,0:T(8,128)(2,1)}), bf16[8,32,32,128]{3,2,1,0:T(8,128)(2,1)}, u32[]{:S(2)}, u32[]{:S(2)}) async-start(bf16[8,32,32,128]{3,2,1,0:T(8,128)(2,1)} %bitcast.34), calls=%async_computation.1 | async-start | bytes 4194304 | tf_op jit(solution)/shard_map/all_to_all | solution.py:302
  31.9 1.9 %collective-permute-start = (bf16[18,3,64,128]{3,2,1,0:T(8,128)(2,1)}, bf16[18,3,64,128]{3,2,1,0:T(8,128)(2,1)S(1)}, u32[]{:S(2)}, u32[]{:S(2)}) collective-permute-start(bf16[18,3,64,128]{3,2,1,0:T(8,128)(2,1)} %pad_maximum_fusion.1), channel_id=1, source_target_pairs={{0,1},{1,2},{2,3},{3,4},{4,5},{5,6},{6,7},{7,8},{8,9},{9,10},{10,1... | collective-permute-start | bytes 2654216 | tf_op jit(solution)/shard_map/ppermute | solution.py:296
  33.9 2.6 %collective-permute-start.1 = (bf16[18,3,64,128]{3,2,1,0:T(8,128)(2,1)}, bf16[18,3,64,128]{3,2,1,0:T(8,128)(2,1)S(1)}, u32[]{:S(2)}, u32[]{:S(2)}) collective-permute-start(bf16[18,3,64,128]{3,2,1,0:T(8,128)(2,1)} %fusion.5), channel_id=1, source_target_pairs={{1,0},{2,1},{3,2},{4,3},{5,4},{6,5},{7,6},{8,7},{9,8},{10,9},{11,1... | collective-permute-start | bytes 2654216 | tf_op jit(solution)/shard_map/ppermute | solution.py:297
  36.4 1.9 %collective-permute-start.3 = (bf16[16,3,64,128]{3,2,1,0:T(8,128)(2,1)}, bf16[16,3,64,128]{3,2,1,0:T(8,128)(2,1)S(1)}, u32[]{:S(2)}, u32[]{:S(2)}) collective-permute-start(bf16[16,3,64,128]{3,2,1,0:T(8,128)(2,1)} %get-tuple-element.16), channel_id=1, source_target_pairs={{1,0},{2,1},{3,2},{4,3},{5,4},{6,5},{7,6},{8,7},{9,8},{10,9},{11,1... | collective-permute-start | bytes 2359304 | tf_op jit(solution)/shard_map/ppermute | solution.py:299
  38.4 3.6 %collective-permute-start.2 = (bf16[16,3,64,128]{3,2,1,0:T(8,128)(2,1)}, bf16[16,3,64,128]{3,2,1,0:T(8,128)(2,1)S(1)}, u32[]{:S(2)}, u32[]{:S(2)}) collective-permute-start(bf16[16,3,64,128]{3,2,1,0:T(8,128)(2,1)} %get-tuple-element.17), channel_id=1, source_target_pairs={{0,1},{1,2},{2,3},{3,4},{4,5},{5,6},{6,7},{7,8},{8,9},{9,10},{10,1... | collective-permute-start | bytes 2359304 | tf_op jit(solution)/shard_map/ppermute | solution.py:298
  42.0 0.1 add_convert_fusion.edge_ref
  42.1 1.1 reduce_sum.18
  43.2 0.9 collective-permute-done.low_ref.low_start_ref
  44.1 4.7 %collective-permute-done.1.high_ref.high_start_ref = bf16[18,3,64,128]{3,2,1,0:T(8,128)(2,1)S(1)} collective-permute-done((bf16[18,3,64,128]{3,2,1,0:T(8,128)(2,1)}, bf16[18,3,64,128]{3,2,1,0:T(8,128)(2,1)S(1)}, u32[]{:S(2)}, u32[]{:S(2)}) %collective-permute-start.1) | collective-permute-done | bytes 884768 | tf_op jit(solution)/shard_map/ppermute | solution.py:297
  48.8 14.1 %diffuse.2 = f32[16,256]{1,0:T(8,128)S(1)} custom-call(f32[2]{0:T(128)S(1)} %add_convert_fusion.edge_ref, f32[32,4,64,128]{3,2,1,0:T(8,128)} %theta_ref.3, bf16[18,3,64,128]{3,2,1,0:T(8,128)(2,1)S(1)} %collective-permute-done.low_ref.low_start_ref, bf16[18,3,64,128]{3,2,1,0:T(8,128)(2,1)S(1)} %collective-permute-done.1.high_ref.high_start_ref, ...), custom_call_target="tpu_custom_call" | custom-call | flops 314572800 | bytes 52428800 | tf_op jit(solution)/shard_map/diffuse/pallas_call | solution.py:116
  62.9 0.0 collective-permute-done.3.high_ref
  62.9 0.0 collective-permute-done.2.low_ref
  62.9 14.1 %diffuse.3 = f32[16,256]{1,0:T(8,128)S(1)} custom-call(f32[2]{0:T(128)S(1)} %add_convert_fusion.edge_ref, f32[32,4,64,128]{3,2,1,0:T(8,128)} %theta_ref.3, bf16[16,3,64,128]{3,2,1,0:T(8,128)(2,1)S(1)} %collective-permute-done.2.low_ref, bf16[16,3,64,128]{3,2,1,0:T(8,128)(2,1)S(1)} %collective-permute-done.3.high_ref, ...), custom_call_target="tpu_custom_call" | custom-call | flops 314572800 | bytes 52428800 | tf_op jit(solution)/shard_map/diffuse/pallas_call | solution.py:116
  77.0 0.0 all-to-all-done.1
  77.1 0.8 broadcast_in_dim.9
  77.9 6.6 %all-to-all-start.2 = ((f32[8,2,32,256]{3,2,1,0:T(8,128)}), f32[8,2,32,256]{3,2,1,0:T(8,128)S(1)}, u32[]{:S(2)}, u32[]{:S(2)}) async-start(f32[8,2,32,256]{3,2,1,0:T(8,128)} %broadcast_in_dim.9), calls=%async_computation.2 | async-start | bytes 1048576 | tf_op jit(solution)/shard_map/all_to_all | solution.py:258
  84.6 3.9 %copy.19 = bf16[32,8,32,128]{3,1,2,0:T(8,128)(2,1)} copy(bf16[32,8,32,128]{3,2,1,0:T(8,128)(2,1)} %bitcast.22) | data formatting | bytes 4194304
  88.5 5.8 %all-to-all-done.2 = f32[8,2,32,256]{3,2,1,0:T(8,128)S(1)} async-done(((f32[8,2,32,256]{3,2,1,0:T(8,128)}), f32[8,2,32,256]{3,2,1,0:T(8,128)S(1)}, u32[]{:S(2)}, u32[]{:S(2)}) %all-to-all-start.2) | async-done | bytes 524320 | tf_op jit(solution)/shard_map/all_to_all | solution.py:258
  94.3 0.7 gram.1
  95.0 16.2 %all_to_all.35 = f32[16,32,256]{2,1,0:T(8,128)S(1)} all-to-all(f32[16,32,256]{2,1,0:T(8,128)S(1)} %gram.1), channel_id=1, replica_groups=mesh['mem'=8,'space'=16] {'space'}, dimensions={0} | all-to-all | bytes 1048576 | tf_op jit(solution)/shard_map/all_to_all | solution.py:321
  111.3 13.5 %all_to_all.36.parts_ref = f32[16,32,256]{2,1,0:T(8,128)S(1)} all-to-all(f32[16,32,256]{2,1,0:T(8,128)S(1)} %broadcast_in_dim.10), channel_id=1, replica_groups=mesh['mem'=8,'space'=16] {'space'}, dimensions={0} | all-to-all | bytes 1048576 | tf_op jit(solution)/shard_map/all_to_all | solution.py:258
  124.8 0.8 broadcast_in_dim.11
  125.7 4.4 %all-to-all-start.6 = ((f32[16,32,256]{2,1,0:T(8,128)}), f32[16,32,256]{2,1,0:T(8,128)S(1)}, u32[]{:S(2)}, u32[]{:S(2)}) async-start(f32[16,32,256]{2,1,0:T(8,128)} %broadcast_in_dim.11), calls=%async_computation.6 | async-start | bytes 1048576 | tf_op jit(solution)/shard_map/all_to_all | solution.py:258
  130.1 9.5 %solve.1.mix_ref = bf16[256,256]{1,0:T(8,128)(2,1)S(1)} custom-call(f32[16,32,256]{2,1,0:T(8,128)S(1)} %all_to_all.36.parts_ref), custom_call_target="tpu_custom_call" | custom-call | flops 1073741824 | bytes 31457280 | tf_op jit(solution)/shard_map/solve/pallas_call | solution.py:328
  139.6 2.3 %shared.1 = bf16[256,4096]{1,0:T(8,128)(2,1)S(1)} custom-call(bf16[256,256]{1,0:T(8,128)(2,1)S(1)} %solve.1.mix_ref, bf16[256,4096]{1,0:T(8,128)(2,1)} %bitcast.42), custom_call_target="tpu_custom_call" | custom-call | tf_op jit(solution)/shard_map/shared/pallas_call | solution.py:341
  141.9 0.0 copy-start
  142.0 1.3 copy-done
  143.3 0.0 all-to-all-done.6
  143.3 3.6 %all-to-all-start.5 = ((bf16[8,32,4096]{2,1,0:T(8,128)(2,1)}), bf16[8,32,4096]{2,1,0:T(8,128)(2,1)S(1)}, u32[]{:S(2)}, u32[]{:S(2)}) async-start(bf16[8,32,4096]{2,1,0:T(8,128)(2,1)} %bitcast.37), calls=%async_computation.5 | async-start | bytes 4194304 | tf_op jit(solution)/shard_map/all_to_all | solution.py:347
  146.9 2.8 %fusion.4 = f32[256,32]{0,1:T(8,128)} fusion(f32[32,4096]{1,0:T(8,128)S(1)} %bitcast.46, s32[256]{0:T(256)S(1)} %dynamic_slice.3), kind=kOutput, calls=%fused_computation.7 | convolution fusion | flops 403709952 | bytes 558080 | tf_op jit(solution)/shard_map/dot_general | solution.py:326
  149.8 23.3 %all-to-all-done.5.change_ref = bf16[8,32,4096]{2,1,0:T(8,128)(2,1)S(1)} async-done(((bf16[8,32,4096]{2,1,0:T(8,128)(2,1)}), bf16[8,32,4096]{2,1,0:T(8,128)(2,1)S(1)}, u32[]{:S(2)}, u32[]{:S(2)}) %all-to-all-start.5) | async-done | bytes 2097184 | tf_op jit(solution)/shard_map/all_to_all | solution.py:347
  173.0 7.0 %finish.1 = f32[32,256,128]{2,1,0:T(8,128)} custom-call(f32[32,256,128]{2,1,0:T(8,128)} %bitcast.41, bf16[8,32,4096]{2,1,0:T(8,128)(2,1)S(1)} %all-to-all-done.5.change_ref), custom_call_target="tpu_custom_call" | custom-call | flops 2097152 | bytes 10485760 | tf_op jit(solution)/shard_map/finish/pallas_call | solution.py:240
  (10 shorter events, 0.2 us)
Async XLA Ops:
  0.6 11.7 %copy-start.1 = (f32[4,64,128]{2,1,0:T(8,128)S(1)}, f32[4,64,128]{2,1,0:T(8,128)}, u32[]{:S(2)}) copy-start(f32[4,64,128]{2,1,0:T(8,128)} %own_start_ref.3) | copy-start | bytes 393220
  5.5 18.2 %all-to-all-start = ((f32[16,40,256]{2,1,0:T(8,128)}), f32[16,40,256]{2,1,0:T(8,128)S(1)}, u32[]{:S(2)}, u32[]{:S(2)}) async-start(f32[16,40,256]{2,1,0:T(8,128)} %bitcast.36), calls=%async_computation | async-start | bytes 1310720 | tf_op jit(solution)/shard_map/all_to_all | solution.py:281
  23.7 0.8 copy-start.2
  24.6 52.5 %all-to-all-start.1 = ((bf16[8,32,32,128]{3,2,1,0:T(8,128)(2,1)}), bf16[8,32,32,128]{3,2,1,0:T(8,128)(2,1)}, u32[]{:S(2)}, u32[]{:S(2)}) async-start(bf16[8,32,32,128]{3,2,1,0:T(8,128)(2,1)} %bitcast.34), calls=%async_computation.1 | async-start | bytes 4194304 | tf_op jit(solution)/shard_map/all_to_all | solution.py:302
  31.9 12.2 %collective-permute-start = (bf16[18,3,64,128]{3,2,1,0:T(8,128)(2,1)}, bf16[18,3,64,128]{3,2,1,0:T(8,128)(2,1)S(1)}, u32[]{:S(2)}, u32[]{:S(2)}) collective-permute-start(bf16[18,3,64,128]{3,2,1,0:T(8,128)(2,1)} %pad_maximum_fusion.1), channel_id=1, source_target_pairs={{0,1},{1,2},{2,3},{3,4},{4,5},{5,6},{6,7},{7,8},{8,9},{9,10},{10,1... | collective-permute-start | bytes 2654216 | tf_op jit(solution)/shard_map/ppermute | solution.py:296
  33.9 15.0 %collective-permute-start.1 = (bf16[18,3,64,128]{3,2,1,0:T(8,128)(2,1)}, bf16[18,3,64,128]{3,2,1,0:T(8,128)(2,1)S(1)}, u32[]{:S(2)}, u32[]{:S(2)}) collective-permute-start(bf16[18,3,64,128]{3,2,1,0:T(8,128)(2,1)} %fusion.5), channel_id=1, source_target_pairs={{1,0},{2,1},{3,2},{4,3},{5,4},{6,5},{7,6},{8,7},{9,8},{10,9},{11,1... | collective-permute-start | bytes 2654216 | tf_op jit(solution)/shard_map/ppermute | solution.py:297
  36.4 26.5 %collective-permute-start.3 = (bf16[16,3,64,128]{3,2,1,0:T(8,128)(2,1)}, bf16[16,3,64,128]{3,2,1,0:T(8,128)(2,1)S(1)}, u32[]{:S(2)}, u32[]{:S(2)}) collective-permute-start(bf16[16,3,64,128]{3,2,1,0:T(8,128)(2,1)} %get-tuple-element.16), channel_id=1, source_target_pairs={{1,0},{2,1},{3,2},{4,3},{5,4},{6,5},{7,6},{8,7},{9,8},{10,9},{11,1... | collective-permute-start | bytes 2359304 | tf_op jit(solution)/shard_map/ppermute | solution.py:299
  38.4 24.6 %collective-permute-start.2 = (bf16[16,3,64,128]{3,2,1,0:T(8,128)(2,1)}, bf16[16,3,64,128]{3,2,1,0:T(8,128)(2,1)S(1)}, u32[]{:S(2)}, u32[]{:S(2)}) collective-permute-start(bf16[16,3,64,128]{3,2,1,0:T(8,128)(2,1)} %get-tuple-element.17), channel_id=1, source_target_pairs={{0,1},{1,2},{2,3},{3,4},{4,5},{5,6},{6,7},{7,8},{8,9},{9,10},{10,1... | collective-permute-start | bytes 2359304 | tf_op jit(solution)/shard_map/ppermute | solution.py:298
  77.9 16.3 %all-to-all-start.2 = ((f32[8,2,32,256]{3,2,1,0:T(8,128)}), f32[8,2,32,256]{3,2,1,0:T(8,128)S(1)}, u32[]{:S(2)}, u32[]{:S(2)}) async-start(f32[8,2,32,256]{3,2,1,0:T(8,128)} %broadcast_in_dim.9), calls=%async_computation.2 | async-start | bytes 1048576 | tf_op jit(solution)/shard_map/all_to_all | solution.py:258
  125.7 17.6 %all-to-all-start.6 = ((f32[16,32,256]{2,1,0:T(8,128)}), f32[16,32,256]{2,1,0:T(8,128)S(1)}, u32[]{:S(2)}, u32[]{:S(2)}) async-start(f32[16,32,256]{2,1,0:T(8,128)} %broadcast_in_dim.11), calls=%async_computation.6 | async-start | bytes 1048576 | tf_op jit(solution)/shard_map/all_to_all | solution.py:258
  141.9 1.3 copy-start
  143.3 29.8 %all-to-all-start.5 = ((bf16[8,32,4096]{2,1,0:T(8,128)(2,1)}), bf16[8,32,4096]{2,1,0:T(8,128)(2,1)S(1)}, u32[]{:S(2)}, u32[]{:S(2)}) async-start(bf16[8,32,4096]{2,1,0:T(8,128)(2,1)} %bitcast.37), calls=%async_computation.5 | async-start | bytes 4194304 | tf_op jit(solution)/shard_map/all_to_all | solution.py:347

commit v3 on v2

--- a/solution.py
+++ b/solution.py
@@ -51,7 +51,7 @@
     def down(v, axis):
         return pltpu.roll(v, 1, axis)
 
-    @pl.loop(0, members)
+    @pl.loop(0, members, unroll=2)
     def _(m):
         def resistance(p):
             if p < width:
@@ -225,22 +225,25 @@
 
 
 def finish_kernel(theta_ref, change_ref, out_ref):
-    members, some, lanes = theta_ref.shape
-    for m in range(0, members, 8):
-        change = change_ref[0, m : m + 8, :].astype(jnp.float32)
-        change = jnp.stack([change[:, r * lanes : (r + 1) * lanes] for r in range(some)])
-        out_ref[m : m + 8] = theta_ref[m : m + 8] + jnp.swapaxes(change, 0, 1)
+    members, _, lanes = theta_ref.shape
+    chunks, _, cells = change_ref.shape
+    some = cells // lanes
+    for c in range(chunks):
+        change = change_ref[c].astype(jnp.float32)
+        rows = slice(c * some, (c + 1) * some)
+        for m in range(0, members, 8):
+            turned = jnp.stack([change[m : m + 8, r * lanes : (r + 1) * lanes] for r in range(some)])
+            out_ref[m : m + 8, rows] = theta_ref[m : m + 8, rows] + jnp.swapaxes(turned, 0, 1)
 
 
 def finish(theta, changes):
     members, rows, lanes = theta.shape
     chunks, _, cells = changes.shape
-    some = cells // lanes
-    block = pl.BlockSpec((members, some, lanes), lambda i: (0, i, 0))
+    block = pl.BlockSpec((members, rows // 2, lanes), lambda i: (0, i, 0))
     return pl.pallas_call(
         finish_kernel,
-        grid=(chunks,),
-        in_specs=[block, pl.BlockSpec((1, members, cells), lambda i: (i, 0, 0))],
+        grid=(2,),
+        in_specs=[block, pl.BlockSpec((chunks // 2, members, cells), lambda i: (i, 0, 0))],
         out_specs=block,
         out_shape=jax.ShapeDtypeStruct(theta.shape, jnp.float32),
         compiler_params=pltpu.CompilerParams(vmem_limit_bytes=50 * MIB),
@@ -338,10 +341,17 @@
         name="solve",
     )(whole)
     factor = 1.0 / math.sqrt(everyone - 1)
+    piece = cells // 2
     changes = pl.pallas_call(
         functools.partial(shared_kernel, factor),
+        grid=(cells // piece,),
+        in_specs=[
+            pl.BlockSpec((everyone, everyone), lambda i: (0, 0)),
+            pl.BlockSpec((everyone, piece), lambda i: (0, i)),
+        ],
+        out_specs=pl.BlockSpec((everyone, piece), lambda i: (0, i)),
         out_shape=jax.ShapeDtypeStruct((everyone, cells), jnp.bfloat16),
-        compiler_params=pltpu.CompilerParams(vmem_limit_bytes=50 * MIB),
+        compiler_params=pltpu.CompilerParams(vmem_limit_bytes=60 * MIB),
         name="shared",
     )(mix, shared)
     changes = lax.all_to_all(changes.reshape(mems, members, cells), "mem", 0, 0)

time: 181 us -> 178 us (0.983)
  Pallas kernels: 47.7 us -> 44.9 us
    pallas_call x2, Pallas kernels: 9.29 us -> 7.27 us  [the longest x1 4.13 us: finish(): pl.pallas_call(finish_kernel, grid=(2,), in_specs=[block, pl.BlockSpec((c...]
  transfers between devices with their start and end apart: 9 -> 9, of which waited for: 5 -> 5; matrix products, arithmetic and copies ran while one was open for 9% -> 9% of each run, Pallas kernels for 22% -> 23%
where the time goes in v3:
time: 178 us; the launch traced here: 177 us
  Pallas kernels  44.9 us (25%)
  starting transfers between devices  38.9 us (22%)
  waiting for transfers between devices  38.2 us (21%)
  blocking collectives  29.3 us (16%)
  local copies, waits for them, and re-layouts  12.4 us (7%)
  other arithmetic  7.47 us (4%)
  matrix products  4.52 us (3%)
    pallas_call x2, Pallas kernels, diffuse(): pl.pallas_call(diffuse_kernel, grid=(members // some,), in_specs=[pl.Bloc...  27.4 us
    all_to_all x1, waiting for transfers between devices, body(): changes = lax.all_to_all(changes.reshape(mems, members, cells), 'mem', 0, 0)  23.3 us
    all_to_all x1, blocking collectives, body(): sums = jnp.sum(lax.all_to_all(partial_sums, 'space', 0, 0), axis=0)  15.8 us
    all_to_all x1, blocking collectives, spread_out(): lax.all_to_all(jnp.broadcast_to(block[None], (count,) + block.shape), axi...  13.5 us
    all_to_all x2, starting transfers between devices, spread_out(): lax.all_to_all(jnp.broadcast_to(block[None], (count,) + block.shape), axi...  11.1 us
    pallas_call x1, Pallas kernels, body(): pl.pallas_call(solve_kernel, out_shape=jax.ShapeDtypeStruct((everyone, ev...  9.53 us
    all_to_all x1, starting transfers between devices, body(): shared = lax.all_to_all(shares, 'mem', 0, 0)  7.37 us
    all_to_all x1, starting transfers between devices, body(): by_line = lax.all_to_all(by_line, 'space', 0, 0)  6.83 us
  transfers between devices with their start and end apart: 9, of which 5 were waited for; matrix products, arithmetic and copies ran while one was open for 9% of the time, Pallas kernels for 23%

profile of v3, /device:TPU:1, one launch (start us, length us, event | category | flops | bytes accessed | tf_op | source)
XLA Modules:
  0.0 176.6 jit_solution(4456311532339347722)
XLA Ops:
  0.6 0.0 copy-start.1
  0.6 0.7 broadcast_divide_fusion
  1.4 0.8 dynamic_slice.3
  2.1 0.8 multiply_bitcast_fusion
  2.9 1.7 fusion.1
  4.6 0.9 copy.21
  5.5 6.8 %all-to-all-start = ((f32[16,40,256]{2,1,0:T(8,128)}), f32[16,40,256]{2,1,0:T(8,128)S(1)}, u32[]{:S(2)}, u32[]{:S(2)}) async-start(f32[16,40,256]{2,1,0:T(8,128)} %bitcast.36), calls=%async_computation | async-start | bytes 1310720 | tf_op jit(solution)/shard_map/all_to_all | solution.py:284
  12.3 0.0 copy-done.1
  12.4 2.7 %convert_element_type.16 = bf16[32,4,64,128]{3,2,1,0:T(8,128)(2,1)S(1)} convert(f32[32,4,64,128]{3,2,1,0:T(8,128)} %theta_ref.3) | non-fusion elementwise | flops 1048576 | bytes 6291456 | tf_op jit(solution)/shard_map/convert_element_type | solution.py:285
  15.1 1.8 copy.20
  16.8 1.8 %fusion.18 = (bf16[16,3,64,128]{3,2,1,0:T(8,128)(2,1)}, bf16[16,3,64,128]{3,2,1,0:T(8,128)(2,1)}, bf16[16,3,64,128]{3,2,1,0:T(8,128)(2,1)S(1)}, bf16[16,3,64,128]{3,2,1,0:T(8,128)(2,1)S(1)}) fusion(bf16[32,4,64,128]{3,2,1,0:T(8,128)(2,1)S(1)} %convert_element_type.16), kind=kLoop, calls=%fused_computation.36 | loop fusion | bytes 6291456 | tf_op jit(solution)/shard_map/slice | solution.py:295
  18.6 1.0 fusion.5
  19.6 1.0 pad_maximum_fusion.1
  20.6 3.1 %all-to-all-done = f32[16,40,256]{2,1,0:T(8,128)S(1)} async-done(((f32[16,40,256]{2,1,0:T(8,128)}), f32[16,40,256]{2,1,0:T(8,128)S(1)}, u32[]{:S(2)}, u32[]{:S(2)}) %all-to-all-start) | async-done | bytes 655392 | tf_op jit(solution)/shard_map/all_to_all | solution.py:284
  23.7 0.0 copy-start.2
  23.7 0.8 copy-done.2
  24.6 7.4 %all-to-all-start.1 = ((bf16[8,32,32,128]{3,2,1,0:T(8,128)(2,1)}), bf16[8,32,32,128]{3,2,1,0:T(8,128)(2,1)}, u32[]{:S(2)}, u32[]{:S(2)}) async-start(bf16[8,32,32,128]{3,2,1,0:T(8,128)(2,1)} %bitcast.34), calls=%async_computation.1 | async-start | bytes 4194304 | tf_op jit(solution)/shard_map/all_to_all | solution.py:305
  31.9 1.9 %collective-permute-start = (bf16[18,3,64,128]{3,2,1,0:T(8,128)(2,1)}, bf16[18,3,64,128]{3,2,1,0:T(8,128)(2,1)S(1)}, u32[]{:S(2)}, u32[]{:S(2)}) collective-permute-start(bf16[18,3,64,128]{3,2,1,0:T(8,128)(2,1)} %pad_maximum_fusion.1), channel_id=1, source_target_pairs={{0,1},{1,2},{2,3},{3,4},{4,5},{5,6},{6,7},{7,8},{8,9},{9,10},{10,1... | collective-permute-start | bytes 2654216 | tf_op jit(solution)/shard_map/ppermute | solution.py:299
  33.9 2.6 %collective-permute-start.1 = (bf16[18,3,64,128]{3,2,1,0:T(8,128)(2,1)}, bf16[18,3,64,128]{3,2,1,0:T(8,128)(2,1)S(1)}, u32[]{:S(2)}, u32[]{:S(2)}) collective-permute-start(bf16[18,3,64,128]{3,2,1,0:T(8,128)(2,1)} %fusion.5), channel_id=1, source_target_pairs={{1,0},{2,1},{3,2},{4,3},{5,4},{6,5},{7,6},{8,7},{9,8},{10,9},{11,1... | collective-permute-start | bytes 2654216 | tf_op jit(solution)/shard_map/ppermute | solution.py:300
  36.4 1.9 %collective-permute-start.3 = (bf16[16,3,64,128]{3,2,1,0:T(8,128)(2,1)}, bf16[16,3,64,128]{3,2,1,0:T(8,128)(2,1)S(1)}, u32[]{:S(2)}, u32[]{:S(2)}) collective-permute-start(bf16[16,3,64,128]{3,2,1,0:T(8,128)(2,1)} %get-tuple-element.16), channel_id=1, source_target_pairs={{1,0},{2,1},{3,2},{4,3},{5,4},{6,5},{7,6},{8,7},{9,8},{10,9},{11,1... | collective-permute-start | bytes 2359304 | tf_op jit(solution)/shard_map/ppermute | solution.py:302
  38.4 3.6 %collective-permute-start.2 = (bf16[16,3,64,128]{3,2,1,0:T(8,128)(2,1)}, bf16[16,3,64,128]{3,2,1,0:T(8,128)(2,1)S(1)}, u32[]{:S(2)}, u32[]{:S(2)}) collective-permute-start(bf16[16,3,64,128]{3,2,1,0:T(8,128)(2,1)} %get-tuple-element.17), channel_id=1, source_target_pairs={{0,1},{1,2},{2,3},{3,4},{4,5},{5,6},{6,7},{7,8},{8,9},{9,10},{10,1... | collective-permute-start | bytes 2359304 | tf_op jit(solution)/shard_map/ppermute | solution.py:301
  42.0 0.1 add_convert_fusion.edge_ref
  42.1 1.1 reduce_sum.18
  43.2 0.9 collective-permute-done.low_ref.low_start_ref
  44.1 4.7 %collective-permute-done.1.high_ref.high_start_ref = bf16[18,3,64,128]{3,2,1,0:T(8,128)(2,1)S(1)} collective-permute-done((bf16[18,3,64,128]{3,2,1,0:T(8,128)(2,1)}, bf16[18,3,64,128]{3,2,1,0:T(8,128)(2,1)S(1)}, u32[]{:S(2)}, u32[]{:S(2)}) %collective-permute-start.1) | collective-permute-done | bytes 884768 | tf_op jit(solution)/shard_map/ppermute | solution.py:300
  48.8 13.7 %diffuse.2 = f32[16,256]{1,0:T(8,128)S(1)} custom-call(f32[2]{0:T(128)S(1)} %add_convert_fusion.edge_ref, f32[32,4,64,128]{3,2,1,0:T(8,128)} %theta_ref.3, bf16[18,3,64,128]{3,2,1,0:T(8,128)(2,1)S(1)} %collective-permute-done.low_ref.low_start_ref, bf16[18,3,64,128]{3,2,1,0:T(8,128)(2,1)S(1)} %collective-permute-done.1.high_ref.high_start_ref, ...), custom_call_target="tpu_custom_call" | custom-call | flops 314572800 | bytes 52428800 | tf_op jit(solution)/shard_map/diffuse/pallas_call | solution.py:116
  62.5 0.0 collective-permute-done.3.high_ref
  62.6 0.0 collective-permute-done.2.low_ref
  62.6 13.7 %diffuse.3 = f32[16,256]{1,0:T(8,128)S(1)} custom-call(f32[2]{0:T(128)S(1)} %add_convert_fusion.edge_ref, f32[32,4,64,128]{3,2,1,0:T(8,128)} %theta_ref.3, bf16[16,3,64,128]{3,2,1,0:T(8,128)(2,1)S(1)} %collective-permute-done.2.low_ref, bf16[16,3,64,128]{3,2,1,0:T(8,128)(2,1)S(1)} %collective-permute-done.3.high_ref, ...), custom_call_target="tpu_custom_call" | custom-call | flops 314572800 | bytes 52428800 | tf_op jit(solution)/shard_map/diffuse/pallas_call | solution.py:116
  76.3 0.0 all-to-all-done.1
  76.3 0.8 broadcast_in_dim.9
  77.2 6.6 %all-to-all-start.2 = ((f32[8,2,32,256]{3,2,1,0:T(8,128)}), f32[8,2,32,256]{3,2,1,0:T(8,128)S(1)}, u32[]{:S(2)}, u32[]{:S(2)}) async-start(f32[8,2,32,256]{3,2,1,0:T(8,128)} %broadcast_in_dim.9), calls=%async_computation.2 | async-start | bytes 1048576 | tf_op jit(solution)/shard_map/all_to_all | solution.py:261
  83.8 3.9 %copy.19 = bf16[32,8,32,128]{3,1,2,0:T(8,128)(2,1)} copy(bf16[32,8,32,128]{3,2,1,0:T(8,128)(2,1)} %bitcast.22) | data formatting | bytes 4194304
  87.7 6.2 %all-to-all-done.2 = f32[8,2,32,256]{3,2,1,0:T(8,128)S(1)} async-done(((f32[8,2,32,256]{3,2,1,0:T(8,128)}), f32[8,2,32,256]{3,2,1,0:T(8,128)S(1)}, u32[]{:S(2)}, u32[]{:S(2)}) %all-to-all-start.2) | async-done | bytes 524320 | tf_op jit(solution)/shard_map/all_to_all | solution.py:261
  94.0 0.7 gram.1
  94.7 15.8 %all_to_all.35 = f32[16,32,256]{2,1,0:T(8,128)S(1)} all-to-all(f32[16,32,256]{2,1,0:T(8,128)S(1)} %gram.1), channel_id=1, replica_groups=mesh['mem'=8,'space'=16] {'space'}, dimensions={0} | all-to-all | bytes 1048576 | tf_op jit(solution)/shard_map/all_to_all | solution.py:324
  110.6 13.5 %all_to_all.36.parts_ref = f32[16,32,256]{2,1,0:T(8,128)S(1)} all-to-all(f32[16,32,256]{2,1,0:T(8,128)S(1)} %broadcast_in_dim.10), channel_id=1, replica_groups=mesh['mem'=8,'space'=16] {'space'}, dimensions={0} | all-to-all | bytes 1048576 | tf_op jit(solution)/shard_map/all_to_all | solution.py:261
  124.1 0.8 broadcast_in_dim.11
  125.0 4.4 %all-to-all-start.6 = ((f32[16,32,256]{2,1,0:T(8,128)}), f32[16,32,256]{2,1,0:T(8,128)S(1)}, u32[]{:S(2)}, u32[]{:S(2)}) async-start(f32[16,32,256]{2,1,0:T(8,128)} %broadcast_in_dim.11), calls=%async_computation.6 | async-start | bytes 1048576 | tf_op jit(solution)/shard_map/all_to_all | solution.py:261
  129.4 9.5 %solve.1.mix_ref = bf16[256,256]{1,0:T(8,128)(2,1)S(1)} custom-call(f32[16,32,256]{2,1,0:T(8,128)S(1)} %all_to_all.36.parts_ref), custom_call_target="tpu_custom_call" | custom-call | flops 1073741824 | bytes 31457280 | tf_op jit(solution)/shard_map/solve/pallas_call | solution.py:331
  138.9 0.0 copy-start
  138.9 0.6 copy-done
  139.6 3.1 %shared.1 = bf16[256,4096]{1,0:T(8,128)(2,1)} custom-call(bf16[256,256]{1,0:T(8,128)(2,1)} %copy-done, bf16[256,4096]{1,0:T(8,128)(2,1)} %bitcast.41), custom_call_target="tpu_custom_call" | custom-call | tf_op jit(solution)/shard_map/shared/pallas_call | solution.py:345
  142.7 0.0 all-to-all-done.6
  142.7 3.6 %all-to-all-start.5 = ((bf16[8,32,4096]{2,1,0:T(8,128)(2,1)}), bf16[8,32,4096]{2,1,0:T(8,128)(2,1)S(1)}, u32[]{:S(2)}, u32[]{:S(2)}) async-start(bf16[8,32,4096]{2,1,0:T(8,128)(2,1)} %bitcast.42), calls=%async_computation.5 | async-start | bytes 4194304 | tf_op jit(solution)/shard_map/all_to_all | solution.py:357
  146.4 2.8 %fusion.4 = f32[256,32]{0,1:T(8,128)} fusion(f32[32,4096]{1,0:T(8,128)S(1)} %bitcast.46, s32[256]{0:T(256)S(1)} %dynamic_slice.3), kind=kOutput, calls=%fused_computation.7 | convolution fusion | flops 403709952 | bytes 558080 | tf_op jit(solution)/shard_map/dot_general | solution.py:329
  149.2 23.3 %all-to-all-done.5.change_ref = bf16[8,32,4096]{2,1,0:T(8,128)(2,1)S(1)} async-done(((bf16[8,32,4096]{2,1,0:T(8,128)(2,1)}), bf16[8,32,4096]{2,1,0:T(8,128)(2,1)S(1)}, u32[]{:S(2)}, u32[]{:S(2)}) %all-to-all-start.5) | async-done | bytes 2097184 | tf_op jit(solution)/shard_map/all_to_all | solution.py:357
  172.5 4.1 %finish.1 = f32[32,256,128]{2,1,0:T(8,128)} custom-call(f32[32,256,128]{2,1,0:T(8,128)} %bitcast.40, bf16[8,32,4096]{2,1,0:T(8,128)(2,1)S(1)} %all-to-all-done.5.change_ref), custom_call_target="tpu_custom_call" | custom-call | flops 2097152 | bytes 10485760 | tf_op jit(solution)/shard_map/finish/pallas_call | solution.py:243
  (10 shorter events, 0.2 us)
Async XLA Ops:
  0.6 11.7 %copy-start.1 = (f32[4,64,128]{2,1,0:T(8,128)S(1)}, f32[4,64,128]{2,1,0:T(8,128)}, u32[]{:S(2)}) copy-start(f32[4,64,128]{2,1,0:T(8,128)} %own_start_ref.3) | copy-start | bytes 393220
  5.5 18.2 %all-to-all-start = ((f32[16,40,256]{2,1,0:T(8,128)}), f32[16,40,256]{2,1,0:T(8,128)S(1)}, u32[]{:S(2)}, u32[]{:S(2)}) async-start(f32[16,40,256]{2,1,0:T(8,128)} %bitcast.36), calls=%async_computation | async-start | bytes 1310720 | tf_op jit(solution)/shard_map/all_to_all | solution.py:284
  23.7 0.8 copy-start.2
  24.6 51.7 %all-to-all-start.1 = ((bf16[8,32,32,128]{3,2,1,0:T(8,128)(2,1)}), bf16[8,32,32,128]{3,2,1,0:T(8,128)(2,1)}, u32[]{:S(2)}, u32[]{:S(2)}) async-start(bf16[8,32,32,128]{3,2,1,0:T(8,128)(2,1)} %bitcast.34), calls=%async_computation.1 | async-start | bytes 4194304 | tf_op jit(solution)/shard_map/all_to_all | solution.py:305
  31.9 12.2 %collective-permute-start = (bf16[18,3,64,128]{3,2,1,0:T(8,128)(2,1)}, bf16[18,3,64,128]{3,2,1,0:T(8,128)(2,1)S(1)}, u32[]{:S(2)}, u32[]{:S(2)}) collective-permute-start(bf16[18,3,64,128]{3,2,1,0:T(8,128)(2,1)} %pad_maximum_fusion.1), channel_id=1, source_target_pairs={{0,1},{1,2},{2,3},{3,4},{4,5},{5,6},{6,7},{7,8},{8,9},{9,10},{10,1... | collective-permute-start | bytes 2654216 | tf_op jit(solution)/shard_map/ppermute | solution.py:299
  33.9 15.0 %collective-permute-start.1 = (bf16[18,3,64,128]{3,2,1,0:T(8,128)(2,1)}, bf16[18,3,64,128]{3,2,1,0:T(8,128)(2,1)S(1)}, u32[]{:S(2)}, u32[]{:S(2)}) collective-permute-start(bf16[18,3,64,128]{3,2,1,0:T(8,128)(2,1)} %fusion.5), channel_id=1, source_target_pairs={{1,0},{2,1},{3,2},{4,3},{5,4},{6,5},{7,6},{8,7},{9,8},{10,9},{11,1... | collective-permute-start | bytes 2654216 | tf_op jit(solution)/shard_map/ppermute | solution.py:300
  36.4 26.1 %collective-permute-start.3 = (bf16[16,3,64,128]{3,2,1,0:T(8,128)(2,1)}, bf16[16,3,64,128]{3,2,1,0:T(8,128)(2,1)S(1)}, u32[]{:S(2)}, u32[]{:S(2)}) collective-permute-start(bf16[16,3,64,128]{3,2,1,0:T(8,128)(2,1)} %get-tuple-element.16), channel_id=1, source_target_pairs={{1,0},{2,1},{3,2},{4,3},{5,4},{6,5},{7,6},{8,7},{9,8},{10,9},{11,1... | collective-permute-start | bytes 2359304 | tf_op jit(solution)/shard_map/ppermute | solution.py:302
  38.4 24.2 %collective-permute-start.2 = (bf16[16,3,64,128]{3,2,1,0:T(8,128)(2,1)}, bf16[16,3,64,128]{3,2,1,0:T(8,128)(2,1)S(1)}, u32[]{:S(2)}, u32[]{:S(2)}) collective-permute-start(bf16[16,3,64,128]{3,2,1,0:T(8,128)(2,1)} %get-tuple-element.17), channel_id=1, source_target_pairs={{0,1},{1,2},{2,3},{3,4},{4,5},{5,6},{6,7},{7,8},{8,9},{9,10},{10,1... | collective-permute-start | bytes 2359304 | tf_op jit(solution)/shard_map/ppermute | solution.py:301
  77.2 16.8 %all-to-all-start.2 = ((f32[8,2,32,256]{3,2,1,0:T(8,128)}), f32[8,2,32,256]{3,2,1,0:T(8,128)S(1)}, u32[]{:S(2)}, u32[]{:S(2)}) async-start(f32[8,2,32,256]{3,2,1,0:T(8,128)} %broadcast_in_dim.9), calls=%async_computation.2 | async-start | bytes 1048576 | tf_op jit(solution)/shard_map/all_to_all | solution.py:261
  125.0 17.7 %all-to-all-start.6 = ((f32[16,32,256]{2,1,0:T(8,128)}), f32[16,32,256]{2,1,0:T(8,128)S(1)}, u32[]{:S(2)}, u32[]{:S(2)}) async-start(f32[16,32,256]{2,1,0:T(8,128)} %broadcast_in_dim.11), calls=%async_computation.6 | async-start | bytes 1048576 | tf_op jit(solution)/shard_map/all_to_all | solution.py:261
  138.9 0.6 copy-start
  142.7 29.8 %all-to-all-start.5 = ((bf16[8,32,4096]{2,1,0:T(8,128)(2,1)}), bf16[8,32,4096]{2,1,0:T(8,128)(2,1)S(1)}, u32[]{:S(2)}, u32[]{:S(2)}) async-start(bf16[8,32,4096]{2,1,0:T(8,128)(2,1)} %bitcast.42), calls=%async_computation.5 | async-start | bytes 4194304 | tf_op jit(solution)/shard_map/all_to_all | solution.py:357

commit v4 on v3

--- a/solution.py
+++ b/solution.py
@@ -324,9 +324,18 @@
     sums = jnp.sum(lax.all_to_all(partial_sums, "space", 0, 0), axis=0)
     whole = spread_out(sums, "space")
 
-    lines_slabs = spread_out(after(lines, whole), "space")
+    lines_slabs = after(lines, whole)[None]
+    owners = mine[None].astype(jnp.int32)
+    early = None
+    for k in (8, 4, 2, 1):
+        other = lax.ppermute(lines_slabs, "space", [(i, i ^ k) for i in range(spaces)])
+        early = other if k == 8 else early
+        lines_slabs = jnp.concatenate([lines_slabs, other], axis=0)
+        owners = jnp.concatenate([owners, owners ^ k])
+    held = (owners[:, None] * lines_here + jnp.arange(lines_here, dtype=jnp.int32)[None, :]).reshape(-1)
     lines_slabs = lines_slabs.transpose(1, 0, 2).reshape(members, spaces * lines_here)
-    predicted = (jnp.dot(lines_slabs, pick.T, precision=HIGH) * scale).T
+    picked = (held[:, None] == sensors_here[None, :]).astype(jnp.float32)
+    predicted = (jnp.dot(lines_slabs, picked, precision=HIGH) * scale).T
 
     mix = pl.pallas_call(
         solve_kernel,
@@ -341,6 +350,7 @@
         name="solve",
     )(whole)
     factor = 1.0 / math.sqrt(everyone - 1)
+    mix = after(mix, early)
     piece = cells // 2
     changes = pl.pallas_call(
         functools.partial(shared_kernel, factor),

time: 178 us -> 175 us (0.983)
  blocking collectives: 29.3 us -> 15.8 us
  waiting for transfers between devices: 38.2 us -> 44.1 us
  starting transfers between devices: 38.9 us -> 44.1 us
    all_to_all x1 -> x0, blocking collectives: 13.5 us -> none  [spread_out(): lax.all_to_all(jnp.broadcast_to(block[None], (count,) + block.shape), axi...]
    all_to_all x1, waiting for transfers between devices: 23.3 us -> 10.9 us  [body(): changes = lax.all_to_all(changes.reshape(mems, members, cells), 'mem', 0, 0)]
    all_to_all x2, waiting for transfers between devices: 6.22 us -> 16.1 us  [spread_out(): lax.all_to_all(jnp.broadcast_to(block[None], (count,) + block.shape), axi...]
    ppermute x0 -> x4, waiting for transfers between devices: none -> 8.38 us  [body(): lax.ppermute(lines_slabs, 'space', [(i, i ^ k) for i in range(spaces)])]
    ppermute x0 -> x4, starting transfers between devices: none -> 5.2 us  [body(): lax.ppermute(lines_slabs, 'space', [(i, i ^ k) for i in range(spaces)])]
    unnamed x7 -> x12, local copies, waits for them, and re-layouts: 5.38 us -> 5.43 us
  transfers between devices with their start and end apart: 9 -> 13, of which waited for: 5 -> 9; matrix products, arithmetic and copies ran while one was open for 9% -> 9% of each run, Pallas kernels for 23% -> 21%
where the time goes in v4:
time: 175 us; the launch traced here: 174 us
  Pallas kernels  45 us (26%)
  starting transfers between devices  44.1 us (25%)
  waiting for transfers between devices  44.1 us (25%)
  blocking collectives  15.8 us (9%)
  local copies, waits for them, and re-layouts  12.5 us (7%)
  other arithmetic  7.8 us (4%)
  matrix products  3.73 us (2%)
    pallas_call x2, Pallas kernels, diffuse(): pl.pallas_call(diffuse_kernel, grid=(members // some,), in_specs=[pl.Bloc...  27.4 us
    all_to_all x2, waiting for transfers between devices, spread_out(): lax.all_to_all(jnp.broadcast_to(block[None], (count,) + block.shape), axi...  16.1 us
    all_to_all x1, blocking collectives, body(): sums = jnp.sum(lax.all_to_all(partial_sums, 'space', 0, 0), axis=0)  15.8 us
    all_to_all x2, starting transfers between devices, spread_out(): lax.all_to_all(jnp.broadcast_to(block[None], (count,) + block.shape), axi...  11.1 us
    all_to_all x1, waiting for transfers between devices, body(): changes = lax.all_to_all(changes.reshape(mems, members, cells), 'mem', 0, 0)  10.9 us
    pallas_call x1, Pallas kernels, body(): pl.pallas_call(solve_kernel, out_shape=jax.ShapeDtypeStruct((everyone, ev...  9.53 us
    ppermute x4, waiting for transfers between devices, body(): lax.ppermute(lines_slabs, 'space', [(i, i ^ k) for i in range(spaces)])  8.38 us
    all_to_all x1, starting transfers between devices, body(): shared = lax.all_to_all(shares, 'mem', 0, 0)  7.37 us
  transfers between devices with their start and end apart: 13, of which 9 were waited for; matrix products, arithmetic and copies ran while one was open for 9% of the time, Pallas kernels for 21%

profile of v4, /device:TPU:1, one launch (start us, length us, event | category | flops | bytes accessed | tf_op | source)
XLA Modules:
  0.0 173.9 jit_solution(9979719331890210197)
XLA Ops:
  0.6 0.7 broadcast_divide_fusion
  1.4 0.8 dynamic_slice.3
  2.1 0.8 multiply_bitcast_fusion
  2.9 1.7 fusion
  4.6 0.9 copy.23
  5.5 6.8 %all-to-all-start = ((f32[16,40,256]{2,1,0:T(8,128)}), f32[16,40,256]{2,1,0:T(8,128)S(1)}, u32[]{:S(2)}, u32[]{:S(2)}) async-start(f32[16,40,256]{2,1,0:T(8,128)} %bitcast.42), calls=%async_computation | async-start | bytes 1310720 | tf_op jit(solution)/shard_map/all_to_all | solution.py:284
  12.4 2.7 %convert_element_type.17 = bf16[32,4,64,128]{3,2,1,0:T(8,128)(2,1)S(1)} convert(f32[32,4,64,128]{3,2,1,0:T(8,128)} %theta_ref.3) | non-fusion elementwise | flops 1048576 | bytes 6291456 | tf_op jit(solution)/shard_map/convert_element_type | solution.py:285
  15.1 1.8 %copy.22 = bf16[32,8,32,128]{3,2,0,1:T(8,128)(2,1)} copy(bf16[32,8,32,128]{3,2,1,0:T(8,128)(2,1)S(1)} %bitcast.45) | data formatting | bytes 4194304 | tf_op jit(solution)/shard_map/reshape | solution.py:297
  16.8 1.8 %fusion.22 = (bf16[16,3,64,128]{3,2,1,0:T(8,128)(2,1)}, bf16[16,3,64,128]{3,2,1,0:T(8,128)(2,1)}, bf16[16,3,64,128]{3,2,1,0:T(8,128)(2,1)S(1)}, bf16[16,3,64,128]{3,2,1,0:T(8,128)(2,1)S(1)}) fusion(bf16[32,4,64,128]{3,2,1,0:T(8,128)(2,1)S(1)} %convert_element_type.17), kind=kLoop, calls=%fused_computation.51 | loop fusion | bytes 6291456 | tf_op jit(solution)/shard_map/slice | solution.py:295
  18.6 1.0 fusion.9
  19.6 1.0 pad_maximum_fusion.1
  20.6 3.2 %all-to-all-done = f32[16,40,256]{2,1,0:T(8,128)S(1)} async-done(((f32[16,40,256]{2,1,0:T(8,128)}), f32[16,40,256]{2,1,0:T(8,128)S(1)}, u32[]{:S(2)}, u32[]{:S(2)}) %all-to-all-start) | async-done | bytes 655392 | tf_op jit(solution)/shard_map/all_to_all | solution.py:284
  23.7 0.8 copy-done.2
  24.6 7.4 %all-to-all-start.1 = ((bf16[8,32,32,128]{3,2,1,0:T(8,128)(2,1)}), bf16[8,32,32,128]{3,2,1,0:T(8,128)(2,1)}, u32[]{:S(2)}, u32[]{:S(2)}) async-start(bf16[8,32,32,128]{3,2,1,0:T(8,128)(2,1)} %bitcast.40), calls=%async_computation.1 | async-start | bytes 4194304 | tf_op jit(solution)/shard_map/all_to_all | solution.py:305
  31.9 1.9 %collective-permute-start = (bf16[18,3,64,128]{3,2,1,0:T(8,128)(2,1)}, bf16[18,3,64,128]{3,2,1,0:T(8,128)(2,1)S(1)}, u32[]{:S(2)}, u32[]{:S(2)}) collective-permute-start(bf16[18,3,64,128]{3,2,1,0:T(8,128)(2,1)} %pad_maximum_fusion.1), channel_id=1, source_target_pairs={{0,1},{1,2},{2,3},{3,4},{4,5},{5,6},{6,7},{7,8},{8,9},{9,10},{10,1... | collective-permute-start | bytes 2654216 | tf_op jit(solution)/shard_map/ppermute | solution.py:299
  33.9 2.6 %collective-permute-start.1 = (bf16[18,3,64,128]{3,2,1,0:T(8,128)(2,1)}, bf16[18,3,64,128]{3,2,1,0:T(8,128)(2,1)S(1)}, u32[]{:S(2)}, u32[]{:S(2)}) collective-permute-start(bf16[18,3,64,128]{3,2,1,0:T(8,128)(2,1)} %fusion.9), channel_id=1, source_target_pairs={{1,0},{2,1},{3,2},{4,3},{5,4},{6,5},{7,6},{8,7},{9,8},{10,9},{11,1... | collective-permute-start | bytes 2654216 | tf_op jit(solution)/shard_map/ppermute | solution.py:300
  36.4 1.9 %collective-permute-start.3 = (bf16[16,3,64,128]{3,2,1,0:T(8,128)(2,1)}, bf16[16,3,64,128]{3,2,1,0:T(8,128)(2,1)S(1)}, u32[]{:S(2)}, u32[]{:S(2)}) collective-permute-start(bf16[16,3,64,128]{3,2,1,0:T(8,128)(2,1)} %get-tuple-element.18), channel_id=1, source_target_pairs={{1,0},{2,1},{3,2},{4,3},{5,4},{6,5},{7,6},{8,7},{9,8},{10,9},{11,1... | collective-permute-start | bytes 2359304 | tf_op jit(solution)/shard_map/ppermute | solution.py:302
  38.3 3.6 %collective-permute-start.2 = (bf16[16,3,64,128]{3,2,1,0:T(8,128)(2,1)}, bf16[16,3,64,128]{3,2,1,0:T(8,128)(2,1)S(1)}, u32[]{:S(2)}, u32[]{:S(2)}) collective-permute-start(bf16[16,3,64,128]{3,2,1,0:T(8,128)(2,1)} %get-tuple-element.19), channel_id=1, source_target_pairs={{0,1},{1,2},{2,3},{3,4},{4,5},{5,6},{6,7},{7,8},{8,9},{9,10},{10,1... | collective-permute-start | bytes 2359304 | tf_op jit(solution)/shard_map/ppermute | solution.py:301
  42.1 1.1 reduce_sum.18
  43.2 0.9 collective-permute-done.low_ref.low_start_ref
  44.1 4.7 %collective-permute-done.1.high_ref.high_start_ref = bf16[18,3,64,128]{3,2,1,0:T(8,128)(2,1)S(1)} collective-permute-done((bf16[18,3,64,128]{3,2,1,0:T(8,128)(2,1)}, bf16[18,3,64,128]{3,2,1,0:T(8,128)(2,1)S(1)}, u32[]{:S(2)}, u32[]{:S(2)}) %collective-permute-start.1) | collective-permute-done | bytes 884768 | tf_op jit(solution)/shard_map/ppermute | solution.py:300
  48.8 13.7 %diffuse.2 = f32[16,256]{1,0:T(8,128)S(1)} custom-call(f32[2]{0:T(128)S(1)} %add_convert_fusion.edge_ref, f32[32,4,64,128]{3,2,1,0:T(8,128)} %theta_ref.3, bf16[18,3,64,128]{3,2,1,0:T(8,128)(2,1)S(1)} %collective-permute-done.low_ref.low_start_ref, bf16[18,3,64,128]{3,2,1,0:T(8,128)(2,1)S(1)} %collective-permute-done.1.high_ref.high_start_ref, ...), custom_call_target="tpu_custom_call" | custom-call | flops 314572800 | bytes 52428800 | tf_op jit(solution)/shard_map/diffuse/pallas_call | solution.py:116
  62.6 13.7 %diffuse.3 = f32[16,256]{1,0:T(8,128)S(1)} custom-call(f32[2]{0:T(128)S(1)} %add_convert_fusion.edge_ref, f32[32,4,64,128]{3,2,1,0:T(8,128)} %theta_ref.3, bf16[16,3,64,128]{3,2,1,0:T(8,128)(2,1)S(1)} %collective-permute-done.2.low_ref, bf16[16,3,64,128]{3,2,1,0:T(8,128)(2,1)S(1)} %collective-permute-done.3.high_ref, ...), custom_call_target="tpu_custom_call" | custom-call | flops 314572800 | bytes 52428800 | tf_op jit(solution)/shard_map/diffuse/pallas_call | solution.py:116
  76.3 0.9 broadcast_in_dim.9
  77.2 6.6 %all-to-all-start.2 = ((f32[8,2,32,256]{3,2,1,0:T(8,128)}), f32[8,2,32,256]{3,2,1,0:T(8,128)S(1)}, u32[]{:S(2)}, u32[]{:S(2)}) async-start(f32[8,2,32,256]{3,2,1,0:T(8,128)} %broadcast_in_dim.9), calls=%async_computation.2 | async-start | bytes 1048576 | tf_op jit(solution)/shard_map/all_to_all | solution.py:261
  83.8 3.9 %copy.21 = bf16[32,8,32,128]{3,1,2,0:T(8,128)(2,1)} copy(bf16[32,8,32,128]{3,2,1,0:T(8,128)(2,1)} %bitcast.24) | data formatting | bytes 4194304
  87.7 6.2 %all-to-all-done.2 = f32[8,2,32,256]{3,2,1,0:T(8,128)S(1)} async-done(((f32[8,2,32,256]{3,2,1,0:T(8,128)}), f32[8,2,32,256]{3,2,1,0:T(8,128)S(1)}, u32[]{:S(2)}, u32[]{:S(2)}) %all-to-all-start.2) | async-done | bytes 524320 | tf_op jit(solution)/shard_map/all_to_all | solution.py:261
  94.0 0.7 gram.1
  94.7 15.8 %all_to_all.30 = f32[16,32,256]{2,1,0:T(8,128)S(1)} all-to-all(f32[16,32,256]{2,1,0:T(8,128)S(1)} %gram.1), channel_id=1, replica_groups=mesh['mem'=8,'space'=16] {'space'}, dimensions={0} | all-to-all | bytes 1048576 | tf_op jit(solution)/shard_map/all_to_all | solution.py:324
  110.6 0.9 broadcast_in_dim.10
  111.4 4.4 %all-to-all-start.4 = ((f32[16,32,256]{2,1,0:T(8,128)}), f32[16,32,256]{2,1,0:T(8,128)S(1)}, u32[]{:S(2)}, u32[]{:S(2)}) async-start(f32[16,32,256]{2,1,0:T(8,128)} %broadcast_in_dim.10), calls=%async_computation.4 | async-start | bytes 1048576 | tf_op jit(solution)/shard_map/all_to_all | solution.py:261
  115.9 9.9 %all-to-all-done.4.parts_ref = f32[16,32,256]{2,1,0:T(8,128)S(1)} async-done(((f32[16,32,256]{2,1,0:T(8,128)}), f32[16,32,256]{2,1,0:T(8,128)S(1)}, u32[]{:S(2)}, u32[]{:S(2)}) %all-to-all-start.4) | async-done | bytes 524320 | tf_op jit(solution)/shard_map/all_to_all | solution.py:261
  125.8 0.9 collective-permute-start.4
  126.7 9.5 %solve.1.mix_ref = bf16[256,256]{1,0:T(8,128)(2,1)S(1)} custom-call(f32[16,32,256]{2,1,0:T(8,128)S(1)} %all-to-all-done.4.parts_ref), custom_call_target="tpu_custom_call" | custom-call | flops 1073741824 | bytes 31457280 | tf_op jit(solution)/shard_map/solve/pallas_call | solution.py:340
  136.3 0.6 copy-done
  136.9 3.2 %shared.1 = bf16[256,4096]{1,0:T(8,128)(2,1)} custom-call(bf16[256,256]{1,0:T(8,128)(2,1)} %copy-done, bf16[256,4096]{1,0:T(8,128)(2,1)} %bitcast.48), custom_call_target="tpu_custom_call" | custom-call | tf_op jit(solution)/shard_map/shared/pallas_call | solution.py:355
  140.1 3.6 %all-to-all-start.5 = ((bf16[8,32,4096]{2,1,0:T(8,128)(2,1)}), bf16[8,32,4096]{2,1,0:T(8,128)(2,1)S(1)}, u32[]{:S(2)}, u32[]{:S(2)}) async-start(bf16[8,32,4096]{2,1,0:T(8,128)(2,1)} %bitcast.47), calls=%async_computation.5 | async-start | bytes 4194304 | tf_op jit(solution)/shard_map/all_to_all | solution.py:367
  143.7 0.1 add_xor_fusion.1
  143.8 0.1 add_xor_fusion.2
  143.9 1.0 collective-permute-start.5
  145.1 3.6 %collective-permute-done.5 = f32[2,32,256]{2,1,0:T(8,128)S(1)} collective-permute-done((f32[2,32,256]{2,1,0:T(8,128)S(1)}, f32[2,32,256]{2,1,0:T(8,128)S(1)}, u32[]{:S(2)}, u32[]{:S(2)}) %collective-permute-start.5) | collective-permute-done | bytes 65568 | tf_op jit(solution)/shard_map/ppermute | solution.py:331
  148.7 0.5 collective-permute-start.6
  149.2 3.7 %collective-permute-done.6 = f32[4,32,256]{2,1,0:T(8,128)S(1)} collective-permute-done((f32[4,32,256]{2,1,0:T(8,128)S(1)}, f32[4,32,256]{2,1,0:T(8,128)S(1)}, u32[]{:S(2)}, u32[]{:S(2)}) %collective-permute-start.6) | collective-permute-done | bytes 131104 | tf_op jit(solution)/shard_map/ppermute | solution.py:331
  152.9 2.8 %collective-permute-start.7 = (f32[8,32,256]{2,1,0:T(8,128)S(1)}, f32[8,32,256]{2,1,0:T(8,128)S(1)}, u32[]{:S(2)}, u32[]{:S(2)}) collective-permute-start(f32[8,32,256]{2,1,0:T(8,128)S(1)} %pad_maximum_fusion.2), channel_id=1, source_target_pairs={{0,1},{1,0},{2,3},{3,2},{4,5},{5,4},{6,7},{7,6},{8,9},{9,8},{10,11... | collective-permute-start | bytes 786440 | tf_op jit(solution)/shard_map/ppermute | solution.py:331
  155.7 1.1 collective-permute-done.7
  156.9 2.0 %fusion.6 = f32[256,32]{0,1:T(8,128)} fusion(f32[32,4096]{1,0:T(8,128)S(1)} %bitcast.57, s32[256]{0:T(256)S(1)} %dynamic_slice.3, s32[4096]{0:T(1024)S(1)} %bitcast.58), kind=kOutput, calls=%fused_computation.9 | convolution fusion | flops 403709952 | bytes 574464 | tf_op jit(solution)/shard_map/dot_general | solution.py:338
  158.9 10.9 %all-to-all-done.5.change_ref = bf16[8,32,4096]{2,1,0:T(8,128)(2,1)S(1)} async-done(((bf16[8,32,4096]{2,1,0:T(8,128)(2,1)}), bf16[8,32,4096]{2,1,0:T(8,128)(2,1)S(1)}, u32[]{:S(2)}, u32[]{:S(2)}) %all-to-all-start.5) | async-done | bytes 2097184 | tf_op jit(solution)/shard_map/all_to_all | solution.py:367
  169.8 4.1 %finish.1 = f32[32,256,128]{2,1,0:T(8,128)} custom-call(f32[32,256,128]{2,1,0:T(8,128)} %bitcast.46, bf16[8,32,4096]{2,1,0:T(8,128)(2,1)S(1)} %all-to-all-done.5.change_ref), custom_call_target="tpu_custom_call" | custom-call | flops 2097152 | bytes 10485760 | tf_op jit(solution)/shard_map/finish/pallas_call | solution.py:243
  (31 shorter events, 0.6 us)
Async XLA Ops:
  0.6 11.7 %copy-start.1 = (f32[4,64,128]{2,1,0:T(8,128)S(1)}, f32[4,64,128]{2,1,0:T(8,128)}, u32[]{:S(2)}) copy-start(f32[4,64,128]{2,1,0:T(8,128)} %own_start_ref.3) | copy-start | bytes 393220
  5.5 18.2 %all-to-all-start = ((f32[16,40,256]{2,1,0:T(8,128)}), f32[16,40,256]{2,1,0:T(8,128)S(1)}, u32[]{:S(2)}, u32[]{:S(2)}) async-start(f32[16,40,256]{2,1,0:T(8,128)} %bitcast.42), calls=%async_computation | async-start | bytes 1310720 | tf_op jit(solution)/shard_map/all_to_all | solution.py:284
  23.7 0.8 copy-start.2
  24.6 51.7 %all-to-all-start.1 = ((bf16[8,32,32,128]{3,2,1,0:T(8,128)(2,1)}), bf16[8,32,32,128]{3,2,1,0:T(8,128)(2,1)}, u32[]{:S(2)}, u32[]{:S(2)}) async-start(bf16[8,32,32,128]{3,2,1,0:T(8,128)(2,1)} %bitcast.40), calls=%async_computation.1 | async-start | bytes 4194304 | tf_op jit(solution)/shard_map/all_to_all | solution.py:305
  31.9 12.2 %collective-permute-start = (bf16[18,3,64,128]{3,2,1,0:T(8,128)(2,1)}, bf16[18,3,64,128]{3,2,1,0:T(8,128)(2,1)S(1)}, u32[]{:S(2)}, u32[]{:S(2)}) collective-permute-start(bf16[18,3,64,128]{3,2,1,0:T(8,128)(2,1)} %pad_maximum_fusion.1), channel_id=1, source_target_pairs={{0,1},{1,2},{2,3},{3,4},{4,5},{5,6},{6,7},{7,8},{8,9},{9,10},{10,1... | collective-permute-start | bytes 2654216 | tf_op jit(solution)/shard_map/ppermute | solution.py:299
  33.9 15.0 %collective-permute-start.1 = (bf16[18,3,64,128]{3,2,1,0:T(8,128)(2,1)}, bf16[18,3,64,128]{3,2,1,0:T(8,128)(2,1)S(1)}, u32[]{:S(2)}, u32[]{:S(2)}) collective-permute-start(bf16[18,3,64,128]{3,2,1,0:T(8,128)(2,1)} %fusion.9), channel_id=1, source_target_pairs={{1,0},{2,1},{3,2},{4,3},{5,4},{6,5},{7,6},{8,7},{9,8},{10,9},{11,1... | collective-permute-start | bytes 2654216 | tf_op jit(solution)/shard_map/ppermute | solution.py:300
  36.4 26.1 %collective-permute-start.3 = (bf16[16,3,64,128]{3,2,1,0:T(8,128)(2,1)}, bf16[16,3,64,128]{3,2,1,0:T(8,128)(2,1)S(1)}, u32[]{:S(2)}, u32[]{:S(2)}) collective-permute-start(bf16[16,3,64,128]{3,2,1,0:T(8,128)(2,1)} %get-tuple-element.18), channel_id=1, source_target_pairs={{1,0},{2,1},{3,2},{4,3},{5,4},{6,5},{7,6},{8,7},{9,8},{10,9},{11,1... | collective-permute-start | bytes 2359304 | tf_op jit(solution)/shard_map/ppermute | solution.py:302
  38.3 24.2 %collective-permute-start.2 = (bf16[16,3,64,128]{3,2,1,0:T(8,128)(2,1)}, bf16[16,3,64,128]{3,2,1,0:T(8,128)(2,1)S(1)}, u32[]{:S(2)}, u32[]{:S(2)}) collective-permute-start(bf16[16,3,64,128]{3,2,1,0:T(8,128)(2,1)} %get-tuple-element.19), channel_id=1, source_target_pairs={{0,1},{1,2},{2,3},{3,4},{4,5},{5,6},{6,7},{7,8},{8,9},{9,10},{10,1... | collective-permute-start | bytes 2359304 | tf_op jit(solution)/shard_map/ppermute | solution.py:301
  77.2 16.8 %all-to-all-start.2 = ((f32[8,2,32,256]{3,2,1,0:T(8,128)}), f32[8,2,32,256]{3,2,1,0:T(8,128)S(1)}, u32[]{:S(2)}, u32[]{:S(2)}) async-start(f32[8,2,32,256]{3,2,1,0:T(8,128)} %broadcast_in_dim.9), calls=%async_computation.2 | async-start | bytes 1048576 | tf_op jit(solution)/shard_map/all_to_all | solution.py:261
  111.4 14.4 %all-to-all-start.4 = ((f32[16,32,256]{2,1,0:T(8,128)}), f32[16,32,256]{2,1,0:T(8,128)S(1)}, u32[]{:S(2)}, u32[]{:S(2)}) async-start(f32[16,32,256]{2,1,0:T(8,128)} %broadcast_in_dim.10), calls=%async_computation.4 | async-start | bytes 1048576 | tf_op jit(solution)/shard_map/all_to_all | solution.py:261
  125.8 11.1 %collective-permute-start.4 = (f32[1,32,256]{2,1,0:T(8,128)S(1)}, f32[1,32,256]{2,1,0:T(8,128)S(1)}, u32[]{:S(2)}, u32[]{:S(2)}) collective-permute-start(f32[1,32,256]{2,1,0:T(8,128)S(1)} %bitcast.51), channel_id=1, source_target_pairs={{0,8},{1,9},{2,10},{3,11},{4,12},{5,13},{6,14},{7,15},{8,0},{9,1},... | collective-permute-start | bytes 98312 | tf_op jit(solution)/shard_map/ppermute | solution.py:331
  136.3 0.7 copy-start
  140.1 29.7 %all-to-all-start.5 = ((bf16[8,32,4096]{2,1,0:T(8,128)(2,1)}), bf16[8,32,4096]{2,1,0:T(8,128)(2,1)S(1)}, u32[]{:S(2)}, u32[]{:S(2)}) async-start(bf16[8,32,4096]{2,1,0:T(8,128)(2,1)} %bitcast.47), calls=%async_computation.5 | async-start | bytes 4194304 | tf_op jit(solution)/shard_map/all_to_all | solution.py:367
  143.9 4.7 %collective-permute-start.5 = (f32[2,32,256]{2,1,0:T(8,128)S(1)}, f32[2,32,256]{2,1,0:T(8,128)S(1)}, u32[]{:S(2)}, u32[]{:S(2)}) collective-permute-start(f32[2,32,256]{2,1,0:T(8,128)S(1)} %pad_maximum_fusion.5), channel_id=1, source_target_pairs={{0,4},{1,5},{2,6},{3,7},{4,0},{5,1},{6,2},{7,3},{8,12},{9,13},{10,... | collective-permute-start | bytes 196616 | tf_op jit(solution)/shard_map/ppermute | solution.py:331
  148.7 4.2 %collective-permute-start.6 = (f32[4,32,256]{2,1,0:T(8,128)S(1)}, f32[4,32,256]{2,1,0:T(8,128)S(1)}, u32[]{:S(2)}, u32[]{:S(2)}) collective-permute-start(f32[4,32,256]{2,1,0:T(8,128)S(1)} %pad_maximum_fusion.3), channel_id=1, source_target_pairs={{0,2},{1,3},{2,0},{3,1},{4,6},{5,7},{6,4},{7,5},{8,10},{9,11},{10,... | collective-permute-start | bytes 393224 | tf_op jit(solution)/shard_map/ppermute | solution.py:331
  152.9 3.9 %collective-permute-start.7 = (f32[8,32,256]{2,1,0:T(8,128)S(1)}, f32[8,32,256]{2,1,0:T(8,128)S(1)}, u32[]{:S(2)}, u32[]{:S(2)}) collective-permute-start(f32[8,32,256]{2,1,0:T(8,128)S(1)} %pad_maximum_fusion.2), channel_id=1, source_target_pairs={{0,1},{1,0},{2,3},{3,2},{4,5},{5,4},{6,7},{7,6},{8,9},{9,8},{10,11... | collective-permute-start | bytes 786440 | tf_op jit(solution)/shard_map/ppermute | solution.py:331

commit v5 on v4

--- a/solution.py
+++ b/solution.py
@@ -288,7 +288,7 @@
     begin = jnp.stack([coarse.astype(jnp.bfloat16), fine])
     forward = [(i, i + 1) for i in range(spaces - 1)]
     backward = [(i + 1, i) for i in range(spaces - 1)]
-    half = members // 2
+    half = members // 4
     top, bottom = slice(planes - width, planes), slice(0, width)
     to_high = jnp.concatenate([low_theta[:half, top], begin[:, top]], axis=0)
     to_low = jnp.concatenate([low_theta[:half, bottom], begin[:, bottom]], axis=0)

time: 175 us -> 186 us (1.063)
  waiting for transfers between devices: 44.1 us -> 52.8 us
    ppermute x1, waiting for transfers between devices: 0.9 us -> 11.1 us  [body(): halo_low = lax.ppermute(to_high, 'space', forward)]
  transfers between devices with their start and end apart: 13 -> 13, of which waited for: 9 -> 9; matrix products, arithmetic and copies ran while one was open for 9% -> 9% of each run, Pallas kernels for 21% -> 20%
where the time goes in v5:
time: 186 us; the launch traced here: 185 us
  waiting for transfers between devices  52.8 us (28%)
  Pallas kernels  44.9 us (24%)
  starting transfers between devices  43.5 us (23%)
  blocking collectives  17.2 us (9%)
  local copies, waits for them, and re-layouts  13.5 us (7%)
  other arithmetic  8.28 us (4%)
  matrix products  3.73 us (2%)
    pallas_call x2, Pallas kernels, diffuse(): pl.pallas_call(diffuse_kernel, grid=(members // some,), in_specs=[pl.Bloc...  27.4 us
    all_to_all x1, blocking collectives, body(): sums = jnp.sum(lax.all_to_all(partial_sums, 'space', 0, 0), axis=0)  17.2 us
    all_to_all x2, waiting for transfers between devices, spread_out(): lax.all_to_all(jnp.broadcast_to(block[None], (count,) + block.shape), axi...  14.6 us
    ppermute x1, waiting for transfers between devices, body(): halo_low = lax.ppermute(to_high, 'space', forward)  11.1 us
    all_to_all x2, starting transfers between devices, spread_out(): lax.all_to_all(jnp.broadcast_to(block[None], (count,) + block.shape), axi...  11.1 us
    all_to_all x1, waiting for transfers between devices, body(): changes = lax.all_to_all(changes.reshape(mems, members, cells), 'mem', 0, 0)  10.9 us
    pallas_call x1, Pallas kernels, body(): pl.pallas_call(solve_kernel, out_shape=jax.ShapeDtypeStruct((everyone, ev...  9.53 us
    ppermute x4, waiting for transfers between devices, body(): lax.ppermute(lines_slabs, 'space', [(i, i ^ k) for i in range(spaces)])  8.38 us
  transfers between devices with their start and end apart: 13, of which 9 were waited for; matrix products, arithmetic and copies ran while one was open for 9% of the time, Pallas kernels for 20%

profile of v5, /device:TPU:1, one launch (start us, length us, event | category | flops | bytes accessed | tf_op | source)
XLA Modules:
  0.0 184.7 jit_solution(6080975237922396921)
XLA Ops:
  0.6 0.7 broadcast_divide_fusion
  1.4 0.8 dynamic_slice.3
  2.1 0.8 multiply_bitcast_fusion
  2.9 1.7 fusion
  4.6 0.9 copy.23
  5.5 6.8 %all-to-all-start = ((f32[16,40,256]{2,1,0:T(8,128)}), f32[16,40,256]{2,1,0:T(8,128)S(1)}, u32[]{:S(2)}, u32[]{:S(2)}) async-start(f32[16,40,256]{2,1,0:T(8,128)} %bitcast.42), calls=%async_computation | async-start | bytes 1310720 | tf_op jit(solution)/shard_map/all_to_all | solution.py:284
  12.4 2.7 %convert_element_type.17 = bf16[32,4,64,128]{3,2,1,0:T(8,128)(2,1)S(1)} convert(f32[32,4,64,128]{3,2,1,0:T(8,128)} %theta_ref.3) | non-fusion elementwise | flops 1048576 | bytes 6291456 | tf_op jit(solution)/shard_map/convert_element_type | solution.py:285
  15.2 1.8 copy.22
  17.0 0.9 fusion.9
  17.8 0.8 pad_maximum_fusion.1
  18.7 2.0 %fusion.22 = (bf16[24,3,64,128]{3,2,1,0:T(8,128)(2,1)}, bf16[24,3,64,128]{3,2,1,0:T(8,128)(2,1)}) fusion(bf16[32,4,64,128]{3,2,1,0:T(8,128)(2,1)S(1)} %convert_element_type.17), kind=kLoop, calls=%fused_computation.51 | loop fusion | bytes 4718592 | tf_op jit(solution)/shard_map/slice | solution.py:295
  20.6 3.1 %all-to-all-done = f32[16,40,256]{2,1,0:T(8,128)S(1)} async-done(((f32[16,40,256]{2,1,0:T(8,128)}), f32[16,40,256]{2,1,0:T(8,128)S(1)}, u32[]{:S(2)}, u32[]{:S(2)}) %all-to-all-start) | async-done | bytes 655392 | tf_op jit(solution)/shard_map/all_to_all | solution.py:284
  23.7 0.9 copy-done.2
  24.6 7.4 %all-to-all-start.1 = ((bf16[8,32,32,128]{3,2,1,0:T(8,128)(2,1)}), bf16[8,32,32,128]{3,2,1,0:T(8,128)(2,1)}, u32[]{:S(2)}, u32[]{:S(2)}) async-start(bf16[8,32,32,128]{3,2,1,0:T(8,128)(2,1)} %bitcast.40), calls=%async_computation.1 | async-start | bytes 4194304 | tf_op jit(solution)/shard_map/all_to_all | solution.py:305
  32.0 1.9 %collective-permute-start.2 = (bf16[24,3,64,128]{3,2,1,0:T(8,128)(2,1)}, bf16[24,3,64,128]{3,2,1,0:T(8,128)(2,1)S(1)}, u32[]{:S(2)}, u32[]{:S(2)}) collective-permute-start(bf16[24,3,64,128]{3,2,1,0:T(8,128)(2,1)} %get-tuple-element.19), channel_id=1, source_target_pairs={{0,1},{1,2},{2,3},{3,4},{4,5},{5,6},{6,7},{7,8},{8,9},{9,10},{10,1... | collective-permute-start | bytes 3538952 | tf_op jit(solution)/shard_map/ppermute | solution.py:301
  33.9 2.6 %collective-permute-start.3 = (bf16[24,3,64,128]{3,2,1,0:T(8,128)(2,1)}, bf16[24,3,64,128]{3,2,1,0:T(8,128)(2,1)S(1)}, u32[]{:S(2)}, u32[]{:S(2)}) collective-permute-start(bf16[24,3,64,128]{3,2,1,0:T(8,128)(2,1)} %get-tuple-element.18), channel_id=1, source_target_pairs={{1,0},{2,1},{3,2},{4,3},{5,4},{6,5},{7,6},{8,7},{9,8},{10,9},{11,1... | collective-permute-start | bytes 3538952 | tf_op jit(solution)/shard_map/ppermute | solution.py:302
  36.5 3.0 %collective-permute-start = (bf16[10,3,64,128]{3,2,1,0:T(8,128)(2,1)}, bf16[10,3,64,128]{3,2,1,0:T(8,128)(2,1)S(1)}, u32[]{:S(2)}, u32[]{:S(2)}) collective-permute-start(bf16[10,3,64,128]{3,2,1,0:T(8,128)(2,1)} %pad_maximum_fusion.1), channel_id=1, source_target_pairs={{0,1},{1,2},{2,3},{3,4},{4,5},{5,6},{6,7},{7,8},{8,9},{9,10},{10,1... | collective-permute-start | bytes 1474568 | tf_op jit(solution)/shard_map/ppermute | solution.py:299
  39.5 1.9 %collective-permute-start.1 = (bf16[10,3,64,128]{3,2,1,0:T(8,128)(2,1)}, bf16[10,3,64,128]{3,2,1,0:T(8,128)(2,1)S(1)}, u32[]{:S(2)}, u32[]{:S(2)}) collective-permute-start(bf16[10,3,64,128]{3,2,1,0:T(8,128)(2,1)} %fusion.9), channel_id=1, source_target_pairs={{1,0},{2,1},{3,2},{4,3},{5,4},{6,5},{7,6},{8,7},{9,8},{10,9},{11,1... | collective-permute-start | bytes 1474568 | tf_op jit(solution)/shard_map/ppermute | solution.py:300
  41.5 11.1 %collective-permute-done.low_ref.low_start_ref = bf16[10,3,64,128]{3,2,1,0:T(8,128)(2,1)S(1)} collective-permute-done((bf16[10,3,64,128]{3,2,1,0:T(8,128)(2,1)}, bf16[10,3,64,128]{3,2,1,0:T(8,128)(2,1)S(1)}, u32[]{:S(2)}, u32[]{:S(2)}) %collective-permute-start) | collective-permute-done | bytes 491552 | tf_op jit(solution)/shard_map/ppermute | solution.py:299
  52.6 4.7 %collective-permute-done.1.high_ref.high_start_ref = bf16[10,3,64,128]{3,2,1,0:T(8,128)(2,1)S(1)} collective-permute-done((bf16[10,3,64,128]{3,2,1,0:T(8,128)(2,1)}, bf16[10,3,64,128]{3,2,1,0:T(8,128)(2,1)S(1)}, u32[]{:S(2)}, u32[]{:S(2)}) %collective-permute-start.1) | collective-permute-done | bytes 491552 | tf_op jit(solution)/shard_map/ppermute | solution.py:300
  57.3 7.5 %diffuse.2 = f32[8,256]{1,0:T(8,128)S(1)} custom-call(f32[2]{0:T(128)S(1)} %add_convert_fusion.edge_ref, f32[32,4,64,128]{3,2,1,0:T(8,128)} %theta_ref.3, bf16[10,3,64,128]{3,2,1,0:T(8,128)(2,1)S(1)} %collective-permute-done.low_ref.low_start_ref, bf16[10,3,64,128]{3,2,1,0:T(8,128)(2,1)S(1)} %collective-permute-done.1.high_ref.high_start_ref, ...), custom_call_target="tpu_custom_call" | custom-call | flops 314572800 | bytes 52428800 | tf_op jit(solution)/shard_map/diffuse/pallas_call | solution.py:116
  64.7 1.2 reduce_sum.18
  65.9 0.6 slice_bitcast_fusion
  66.5 19.9 %diffuse.3 = f32[24,256]{1,0:T(8,128)S(1)} custom-call(f32[2]{0:T(128)S(1)} %add_convert_fusion.edge_ref, f32[32,4,64,128]{3,2,1,0:T(8,128)} %theta_ref.3, bf16[24,3,64,128]{3,2,1,0:T(8,128)(2,1)S(1)} %collective-permute-done.2.low_ref, bf16[24,3,64,128]{3,2,1,0:T(8,128)(2,1)S(1)} %collective-permute-done.3.high_ref, ...), custom_call_target="tpu_custom_call" | custom-call | flops 314572800 | bytes 52428800 | tf_op jit(solution)/shard_map/diffuse/pallas_call | solution.py:116
  86.5 0.8 pad_maximum_fusion.4
  87.3 0.8 broadcast_in_dim.9
  88.1 6.6 %all-to-all-start.2 = ((f32[8,2,32,256]{3,2,1,0:T(8,128)}), f32[8,2,32,256]{3,2,1,0:T(8,128)S(1)}, u32[]{:S(2)}, u32[]{:S(2)}) async-start(f32[8,2,32,256]{3,2,1,0:T(8,128)} %broadcast_in_dim.9), calls=%async_computation.2 | async-start | bytes 1048576 | tf_op jit(solution)/shard_map/all_to_all | solution.py:261
  94.8 3.9 %copy.21 = bf16[32,8,32,128]{3,1,2,0:T(8,128)(2,1)} copy(bf16[32,8,32,128]{3,2,1,0:T(8,128)(2,1)} %bitcast.24) | data formatting | bytes 4194304
  98.7 4.7 %all-to-all-done.2 = f32[8,2,32,256]{3,2,1,0:T(8,128)S(1)} async-done(((f32[8,2,32,256]{3,2,1,0:T(8,128)}), f32[8,2,32,256]{3,2,1,0:T(8,128)S(1)}, u32[]{:S(2)}, u32[]{:S(2)}) %all-to-all-start.2) | async-done | bytes 524320 | tf_op jit(solution)/shard_map/all_to_all | solution.py:261
  103.4 0.7 gram.1
  104.2 17.2 %all_to_all.30 = f32[16,32,256]{2,1,0:T(8,128)S(1)} all-to-all(f32[16,32,256]{2,1,0:T(8,128)S(1)} %gram.1), channel_id=1, replica_groups=mesh['mem'=8,'space'=16] {'space'}, dimensions={0} | all-to-all | bytes 1048576 | tf_op jit(solution)/shard_map/all_to_all | solution.py:324
  121.5 0.9 broadcast_in_dim.10
  122.3 4.4 %all-to-all-start.4 = ((f32[16,32,256]{2,1,0:T(8,128)}), f32[16,32,256]{2,1,0:T(8,128)S(1)}, u32[]{:S(2)}, u32[]{:S(2)}) async-start(f32[16,32,256]{2,1,0:T(8,128)} %broadcast_in_dim.10), calls=%async_computation.4 | async-start | bytes 1048576 | tf_op jit(solution)/shard_map/all_to_all | solution.py:261
  126.8 9.9 %all-to-all-done.4.parts_ref = f32[16,32,256]{2,1,0:T(8,128)S(1)} async-done(((f32[16,32,256]{2,1,0:T(8,128)}), f32[16,32,256]{2,1,0:T(8,128)S(1)}, u32[]{:S(2)}, u32[]{:S(2)}) %all-to-all-start.4) | async-done | bytes 524320 | tf_op jit(solution)/shard_map/all_to_all | solution.py:261
  136.7 0.9 collective-permute-start.4
  137.6 9.5 %solve.1.mix_ref = bf16[256,256]{1,0:T(8,128)(2,1)S(1)} custom-call(f32[16,32,256]{2,1,0:T(8,128)S(1)} %all-to-all-done.4.parts_ref), custom_call_target="tpu_custom_call" | custom-call | flops 1073741824 | bytes 31457280 | tf_op jit(solution)/shard_map/solve/pallas_call | solution.py:340
  147.1 0.6 copy-done
  147.8 3.1 %shared.1 = bf16[256,4096]{1,0:T(8,128)(2,1)} custom-call(bf16[256,256]{1,0:T(8,128)(2,1)} %copy-done, bf16[256,4096]{1,0:T(8,128)(2,1)} %bitcast.48), custom_call_target="tpu_custom_call" | custom-call | tf_op jit(solution)/shard_map/shared/pallas_call | solution.py:355
  150.9 3.6 %all-to-all-start.5 = ((bf16[8,32,4096]{2,1,0:T(8,128)(2,1)}), bf16[8,32,4096]{2,1,0:T(8,128)(2,1)S(1)}, u32[]{:S(2)}, u32[]{:S(2)}) async-start(bf16[8,32,4096]{2,1,0:T(8,128)(2,1)} %bitcast.47), calls=%async_computation.5 | async-start | bytes 4194304 | tf_op jit(solution)/shard_map/all_to_all | solution.py:367
  154.8 1.0 collective-permute-start.5
  155.9 3.6 %collective-permute-done.5 = f32[2,32,256]{2,1,0:T(8,128)S(1)} collective-permute-done((f32[2,32,256]{2,1,0:T(8,128)S(1)}, f32[2,32,256]{2,1,0:T(8,128)S(1)}, u32[]{:S(2)}, u32[]{:S(2)}) %collective-permute-start.5) | collective-permute-done | bytes 65568 | tf_op jit(solution)/shard_map/ppermute | solution.py:331
  159.5 0.5 collective-permute-start.6
  160.0 3.7 %collective-permute-done.6 = f32[4,32,256]{2,1,0:T(8,128)S(1)} collective-permute-done((f32[4,32,256]{2,1,0:T(8,128)S(1)}, f32[4,32,256]{2,1,0:T(8,128)S(1)}, u32[]{:S(2)}, u32[]{:S(2)}) %collective-permute-start.6) | collective-permute-done | bytes 131104 | tf_op jit(solution)/shard_map/ppermute | solution.py:331
  163.7 2.8 %collective-permute-start.7 = (f32[8,32,256]{2,1,0:T(8,128)S(1)}, f32[8,32,256]{2,1,0:T(8,128)S(1)}, u32[]{:S(2)}, u32[]{:S(2)}) collective-permute-start(f32[8,32,256]{2,1,0:T(8,128)S(1)} %pad_maximum_fusion.2), channel_id=1, source_target_pairs={{0,1},{1,0},{2,3},{3,2},{4,5},{5,4},{6,7},{7,6},{8,9},{9,8},{10,11... | collective-permute-start | bytes 786440 | tf_op jit(solution)/shard_map/ppermute | solution.py:331
  166.5 1.1 collective-permute-done.7
  167.7 2.0 %fusion.6 = f32[256,32]{0,1:T(8,128)} fusion(f32[32,4096]{1,0:T(8,128)S(1)} %bitcast.57, s32[256]{0:T(256)S(1)} %dynamic_slice.3, s32[4096]{0:T(1024)S(1)} %bitcast.58), kind=kOutput, calls=%fused_computation.9 | convolution fusion | flops 403709952 | bytes 574464 | tf_op jit(solution)/shard_map/dot_general | solution.py:338
  169.8 10.9 %all-to-all-done.5.change_ref = bf16[8,32,4096]{2,1,0:T(8,128)(2,1)S(1)} async-done(((bf16[8,32,4096]{2,1,0:T(8,128)(2,1)}), bf16[8,32,4096]{2,1,0:T(8,128)(2,1)S(1)}, u32[]{:S(2)}, u32[]{:S(2)}) %all-to-all-start.5) | async-done | bytes 2097184 | tf_op jit(solution)/shard_map/all_to_all | solution.py:367
  180.6 4.1 %finish.1 = f32[32,256,128]{2,1,0:T(8,128)} custom-call(f32[32,256,128]{2,1,0:T(8,128)} %bitcast.46, bf16[8,32,4096]{2,1,0:T(8,128)(2,1)S(1)} %all-to-all-done.5.change_ref), custom_call_target="tpu_custom_call" | custom-call | flops 2097152 | bytes 10485760 | tf_op jit(solution)/shard_map/finish/pallas_call | solution.py:243
  (32 shorter events, 0.9 us)
Async XLA Ops:
  0.6 11.7 %copy-start.1 = (f32[4,64,128]{2,1,0:T(8,128)S(1)}, f32[4,64,128]{2,1,0:T(8,128)}, u32[]{:S(2)}) copy-start(f32[4,64,128]{2,1,0:T(8,128)} %own_start_ref.3) | copy-start | bytes 393220
  5.5 18.2 %all-to-all-start = ((f32[16,40,256]{2,1,0:T(8,128)}), f32[16,40,256]{2,1,0:T(8,128)S(1)}, u32[]{:S(2)}, u32[]{:S(2)}) async-start(f32[16,40,256]{2,1,0:T(8,128)} %bitcast.42), calls=%async_computation | async-start | bytes 1310720 | tf_op jit(solution)/shard_map/all_to_all | solution.py:284
  23.7 0.9 copy-start.2
  24.6 61.9 %all-to-all-start.1 = ((bf16[8,32,32,128]{3,2,1,0:T(8,128)(2,1)}), bf16[8,32,32,128]{3,2,1,0:T(8,128)(2,1)}, u32[]{:S(2)}, u32[]{:S(2)}) async-start(bf16[8,32,32,128]{3,2,1,0:T(8,128)(2,1)} %bitcast.40), calls=%async_computation.1 | async-start | bytes 4194304 | tf_op jit(solution)/shard_map/all_to_all | solution.py:305
  32.0 34.6 %collective-permute-start.2 = (bf16[24,3,64,128]{3,2,1,0:T(8,128)(2,1)}, bf16[24,3,64,128]{3,2,1,0:T(8,128)(2,1)S(1)}, u32[]{:S(2)}, u32[]{:S(2)}) collective-permute-start(bf16[24,3,64,128]{3,2,1,0:T(8,128)(2,1)} %get-tuple-element.19), channel_id=1, source_target_pairs={{0,1},{1,2},{2,3},{3,4},{4,5},{5,6},{6,7},{7,8},{8,9},{9,10},{10,1... | collective-permute-start | bytes 3538952 | tf_op jit(solution)/shard_map/ppermute | solution.py:301
  33.9 32.6 %collective-permute-start.3 = (bf16[24,3,64,128]{3,2,1,0:T(8,128)(2,1)}, bf16[24,3,64,128]{3,2,1,0:T(8,128)(2,1)S(1)}, u32[]{:S(2)}, u32[]{:S(2)}) collective-permute-start(bf16[24,3,64,128]{3,2,1,0:T(8,128)(2,1)} %get-tuple-element.18), channel_id=1, source_target_pairs={{1,0},{2,1},{3,2},{4,3},{5,4},{6,5},{7,6},{8,7},{9,8},{10,9},{11,1... | collective-permute-start | bytes 3538952 | tf_op jit(solution)/shard_map/ppermute | solution.py:302
  36.5 16.1 %collective-permute-start = (bf16[10,3,64,128]{3,2,1,0:T(8,128)(2,1)}, bf16[10,3,64,128]{3,2,1,0:T(8,128)(2,1)S(1)}, u32[]{:S(2)}, u32[]{:S(2)}) collective-permute-start(bf16[10,3,64,128]{3,2,1,0:T(8,128)(2,1)} %pad_maximum_fusion.1), channel_id=1, source_target_pairs={{0,1},{1,2},{2,3},{3,4},{4,5},{5,6},{6,7},{7,8},{8,9},{9,10},{10,1... | collective-permute-start | bytes 1474568 | tf_op jit(solution)/shard_map/ppermute | solution.py:299
  39.5 17.8 %collective-permute-start.1 = (bf16[10,3,64,128]{3,2,1,0:T(8,128)(2,1)}, bf16[10,3,64,128]{3,2,1,0:T(8,128)(2,1)S(1)}, u32[]{:S(2)}, u32[]{:S(2)}) collective-permute-start(bf16[10,3,64,128]{3,2,1,0:T(8,128)(2,1)} %fusion.9), channel_id=1, source_target_pairs={{1,0},{2,1},{3,2},{4,3},{5,4},{6,5},{7,6},{8,7},{9,8},{10,9},{11,1... | collective-permute-start | bytes 1474568 | tf_op jit(solution)/shard_map/ppermute | solution.py:300
  88.1 15.3 %all-to-all-start.2 = ((f32[8,2,32,256]{3,2,1,0:T(8,128)}), f32[8,2,32,256]{3,2,1,0:T(8,128)S(1)}, u32[]{:S(2)}, u32[]{:S(2)}) async-start(f32[8,2,32,256]{3,2,1,0:T(8,128)} %broadcast_in_dim.9), calls=%async_computation.2 | async-start | bytes 1048576 | tf_op jit(solution)/shard_map/all_to_all | solution.py:261
  122.3 14.4 %all-to-all-start.4 = ((f32[16,32,256]{2,1,0:T(8,128)}), f32[16,32,256]{2,1,0:T(8,128)S(1)}, u32[]{:S(2)}, u32[]{:S(2)}) async-start(f32[16,32,256]{2,1,0:T(8,128)} %broadcast_in_dim.10), calls=%async_computation.4 | async-start | bytes 1048576 | tf_op jit(solution)/shard_map/all_to_all | solution.py:261
  136.7 11.1 %collective-permute-start.4 = (f32[1,32,256]{2,1,0:T(8,128)S(1)}, f32[1,32,256]{2,1,0:T(8,128)S(1)}, u32[]{:S(2)}, u32[]{:S(2)}) collective-permute-start(f32[1,32,256]{2,1,0:T(8,128)S(1)} %bitcast.51), channel_id=1, source_target_pairs={{0,8},{1,9},{2,10},{3,11},{4,12},{5,13},{6,14},{7,15},{8,0},{9,1},... | collective-permute-start | bytes 98312 | tf_op jit(solution)/shard_map/ppermute | solution.py:331
  147.1 0.6 copy-start
  150.9 29.7 %all-to-all-start.5 = ((bf16[8,32,4096]{2,1,0:T(8,128)(2,1)}), bf16[8,32,4096]{2,1,0:T(8,128)(2,1)S(1)}, u32[]{:S(2)}, u32[]{:S(2)}) async-start(bf16[8,32,4096]{2,1,0:T(8,128)(2,1)} %bitcast.47), calls=%async_computation.5 | async-start | bytes 4194304 | tf_op jit(solution)/shard_map/all_to_all | solution.py:367
  154.8 4.7 %collective-permute-start.5 = (f32[2,32,256]{2,1,0:T(8,128)S(1)}, f32[2,32,256]{2,1,0:T(8,128)S(1)}, u32[]{:S(2)}, u32[]{:S(2)}) collective-permute-start(f32[2,32,256]{2,1,0:T(8,128)S(1)} %pad_maximum_fusion.5), channel_id=1, source_target_pairs={{0,4},{1,5},{2,6},{3,7},{4,0},{5,1},{6,2},{7,3},{8,12},{9,13},{10,... | collective-permute-start | bytes 196616 | tf_op jit(solution)/shard_map/ppermute | solution.py:331
  159.5 4.2 %collective-permute-start.6 = (f32[4,32,256]{2,1,0:T(8,128)S(1)}, f32[4,32,256]{2,1,0:T(8,128)S(1)}, u32[]{:S(2)}, u32[]{:S(2)}) collective-permute-start(f32[4,32,256]{2,1,0:T(8,128)S(1)} %pad_maximum_fusion.3), channel_id=1, source_target_pairs={{0,2},{1,3},{2,0},{3,1},{4,6},{5,7},{6,4},{7,5},{8,10},{9,11},{10,... | collective-permute-start | bytes 393224 | tf_op jit(solution)/shard_map/ppermute | solution.py:331
  163.7 3.9 %collective-permute-start.7 = (f32[8,32,256]{2,1,0:T(8,128)S(1)}, f32[8,32,256]{2,1,0:T(8,128)S(1)}, u32[]{:S(2)}, u32[]{:S(2)}) collective-permute-start(f32[8,32,256]{2,1,0:T(8,128)S(1)} %pad_maximum_fusion.2), channel_id=1, source_target_pairs={{0,1},{1,0},{2,3},{3,2},{4,5},{5,4},{6,7},{7,6},{8,9},{9,8},{10,11... | collective-permute-start | bytes 786440 | tf_op jit(solution)/shard_map/ppermute | solution.py:331
